TPU v7x, 128 devices: a whole 4x4x4 slice. The times are simulated.
128 devices in a mesh: dp: 4 (over z), ctx: 32 (over y, x, core).
Axes of the slice: x: 4, y: 4, z: 4, core: 2. Of those that a mesh axis runs over, the one named last changes fastest.
Arguments:
- queries: bfloat16 [32768, 4096], P(('dp', 'ctx')), may hold values from -27 to 27
- keys: bfloat16 [32768, 512], P(('dp', 'ctx')), may hold values from -9 to 9
- values: bfloat16 [32768, 512], P(('dp', 'ctx')), may hold values from -6 to 6
- upstream: bfloat16 [32768, 4096], P(('dp', 'ctx')), may hold values from -24 to 24
- ancestors: int32 [256, 6], P(('dp', 'ctx')), may hold values from -1 to 63, as said below
- segments: int32 [32768], P(('dp', 'ctx')), may hold values from -1 to 2, as said below
- responses: int32 [32768], P(('dp', 'ctx')), may hold values from -1 to 15, as said below
- rewards: int32 [64], P('dp'), may hold values from 0 to 4, as said below
- lengths: int32 [64], P('dp'), may hold values from 64 to 1024, as said below
Outputs:
- attended: bfloat16 [32768, 4096], P(('dp', 'ctx'))
- grad_q: bfloat16 [32768, 4096], P(('dp', 'ctx'))
- grad_k: float32 [32768, 512], P(('dp', 'ctx'))
- grad_v: float32 [32768, 512], P(('dp', 'ctx'))
Inputs may be any that keep to these rules, and one draw needn't show every extreme that they name: `ancestors`: row b lists the ancestor blocks of block b by their index among the 64 blocks of its group, which lie 2 to a device along ctx in order; unused slots hold -1 and come last. A group's prompt is the 2 blocks of one device: its block number j lists prompt blocks 0 to j - 1. Every other block lists the 2 prompt blocks in its first 2 slots and then k response blocks, 0 <= k <= 4, the one in slot 2 + u lying on the device k - u places before the block's own device along ctx, cyclically; in every group some block has k = 4. All tokens of a listed block have segment 0. `segments`: -1 marks padding at a block's end, 0 the part that continues the block's ancestors, 1 and 2 later leaves branching off segment 0. `responses`: -1 for prompt and padding tokens, else the response within the token's group. `rewards`: in some groups all responses but one share a reward and that one is higher by one. `lengths`: lengths in group number g lie between 128 // 2 * (g + 1) and 2 * 128 * (g + 1).
All inputs are finite; a program needn't handle non-finite values.
Results may differ from a plain program's by a relative error of at most 0.012.
The roundings to bfloat16 on the way count: a program that leaves them out, or rounds other values in their place, can miss the bound.
Values may be sent and summed in bfloat16 or wider, within the bound.
A program may use at most 128 MiB of HBM per device.

v0:
```python
import math

import jax
import jax.numpy as jnp
from jax import lax
from jax.sharding import PartitionSpec as P

HEAD_WIDTH = 128


def from_root(array, axis, root):
    mine = lax.axis_index(axis) == root
    return lax.psum(jnp.where(mine, array, jnp.zeros_like(array)), axis)


def from_behind(array, axis, by):
    size = lax.axis_size(axis)
    return lax.ppermute(array, axis, [(i, (i + by) % size) for i in range(size)])


def visibility(seg_row, slot_valid):
    rows = jnp.arange(seg_row.shape[0])
    earlier = rows[None, :] <= rows[:, None]
    related = (seg_row[None, :] == seg_row[:, None]) | (seg_row[None, :] == 0)
    own_block = earlier & (seg_row[:, None] >= 0) & related | (rows[None, :] == rows[:, None])
    width = seg_row.shape[0]
    remote = jnp.broadcast_to(slot_valid[None, :, None], (width, slot_valid.shape[0], width))
    return jnp.concatenate([remote, own_block[:, None, :]], axis=1)


def block_step(query_block, slot_keys, slot_values, visible, up_block, weight_block):
    inv_root = 1.0 / math.sqrt(query_block.shape[-1])
    scores = (
        jnp.einsum("ihgd,sjhd->hgisj", query_block, slot_keys, preferred_element_type=jnp.float32)
        * inv_root
    )
    masked = jnp.where(visible[None, None], scores, -jnp.inf)
    peak = jnp.max(masked, axis=(3, 4), keepdims=True)
    exponent = jnp.exp(masked - peak)
    denominator = jnp.sum(exponent, axis=(3, 4), keepdims=True)
    probability = exponent / denominator
    prob_low = probability.astype(jnp.bfloat16)
    attended = jnp.einsum(
        "hgisj,sjhd->ihgd", prob_low, slot_values, preferred_element_type=jnp.float32
    ).astype(jnp.bfloat16)
    grad_out = (
        (up_block.astype(jnp.float32) * weight_block[:, None])
        .astype(jnp.bfloat16)
        .reshape(query_block.shape)
    )
    delta = jnp.sum(
        lax.optimization_barrier(grad_out).astype(jnp.float32)
        * lax.optimization_barrier(attended).astype(jnp.float32),
        axis=-1,
    )
    delta = jnp.transpose(delta, (1, 2, 0))[..., None, None]
    dprobs = jnp.einsum(
        "ihgd,sjhd->hgisj", grad_out, slot_values, preferred_element_type=jnp.float32
    )
    dscores = (probability * (dprobs - delta) * inv_root).astype(jnp.bfloat16)
    grad_query = jnp.einsum(
        "hgisj,sjhd->ihgd", dscores, slot_keys, preferred_element_type=jnp.float32
    ).astype(jnp.bfloat16)
    grad_keys = jnp.einsum(
        "hgisj,ihgd->sjhd", dscores, query_block, preferred_element_type=jnp.float32
    )
    grad_values = jnp.einsum(
        "hgisj,ihgd->sjhd", prob_low, grad_out, preferred_element_type=jnp.float32
    )
    return (attended, grad_query, grad_keys, grad_values)


def body(queries, keys, values, upstream, ancestors, segments, responses, rewards, lengths):
    local_blocks = ancestors.shape[0]
    slot_count = ancestors.shape[1]
    block_rows = queries.shape[0] // local_blocks
    kv_heads = keys.shape[1] // HEAD_WIDTH
    query_heads = queries.shape[1] // HEAD_WIDTH
    group_members = query_heads // kv_heads
    reach = slot_count - local_blocks
    ctx_count = lax.axis_size("ctx")
    position = lax.axis_index("ctx")
    total = lax.psum(jnp.sum(lengths.astype(jnp.float32)), "dp")
    scored = rewards.astype(jnp.float32)
    centre = jnp.mean(scored)
    spread = jnp.sqrt(jnp.mean(jnp.square(scored - centre)))
    advantage = (scored - centre) / jnp.maximum(spread, 0.5)
    scale = lax.axis_size("dp") * rewards.shape[0] * block_rows / total
    chosen = responses[:, None] == jnp.arange(rewards.shape[0])[None, :]
    weight = jnp.sum(jnp.where(chosen, advantage[None, :], 0.0), axis=1) * scale
    first_slot = ancestors[0, 0]
    root = jnp.where(first_slot < 0, position, first_slot // local_blocks)
    prompt_keys, prompt_values = (from_root(keys, "ctx", root), from_root(values, "ctx", root))
    key_parts = [keys, prompt_keys]
    value_parts = [values, prompt_values]
    for distance in range(1, reach + 1):
        moved = from_behind((keys, values), "ctx", distance)
        key_parts.append(moved[0])
        value_parts.append(moved[1])
    pool_keys = jnp.concatenate(key_parts, axis=0).reshape(-1, block_rows, kv_heads, HEAD_WIDTH)
    pool_values = jnp.concatenate(value_parts, axis=0).reshape(-1, block_rows, kv_heads, HEAD_WIDTH)
    pool_size = pool_keys.shape[0]
    slots = jnp.arange(slot_count)[None, :]
    owner_gap = (position - ancestors // local_blocks) % ctx_count
    pool_slot = jnp.where(
        slots < local_blocks,
        local_blocks + slots,
        (1 + owner_gap) * local_blocks + ancestors % local_blocks,
    )
    slot_valid = ancestors >= 0
    pool_slot = jnp.where(slot_valid, pool_slot, 0)

    def visit(carry, inputs):
        key_grads, value_grads = carry
        query_block, up_block, weight_block, seg_row, slot_row, valid_row, number = inputs
        members = jnp.concatenate([slot_row, number[None]])
        valid_all = jnp.concatenate([valid_row, jnp.ones((1,), bool)])
        visible = visibility(seg_row, valid_row)
        attended, grad_query, grad_key, grad_value = block_step(
            query_block, pool_keys[members], pool_values[members], visible, up_block, weight_block
        )
        placement = (
            (members[:, None] == jnp.arange(pool_size)[None, :]) & valid_all[:, None]
        ).astype(jnp.float32)
        key_grads = key_grads + jnp.einsum(
            "sp,sjhd->pjhd", placement, grad_key, precision=lax.Precision.HIGHEST
        )
        value_grads = value_grads + jnp.einsum(
            "sp,sjhd->pjhd", placement, grad_value, precision=lax.Precision.HIGHEST
        )
        return ((key_grads, value_grads), (attended, grad_query))

    inputs = (
        queries.reshape(local_blocks, block_rows, kv_heads, group_members, HEAD_WIDTH),
        upstream.reshape(local_blocks, block_rows, query_heads * HEAD_WIDTH),
        weight.reshape(local_blocks, block_rows),
        segments.reshape(local_blocks, block_rows),
        pool_slot,
        slot_valid,
        jnp.arange(local_blocks, dtype=jnp.int32),
    )
    zero_filled = jnp.zeros((pool_size, block_rows, kv_heads, HEAD_WIDTH), jnp.float32)
    (key_grads, value_grads), (attended, grad_query) = lax.scan(
        visit, (zero_filled, zero_filled), inputs
    )
    prompt_sum = lax.psum(
        (key_grads[local_blocks : 2 * local_blocks], value_grads[local_blocks : 2 * local_blocks]),
        "ctx",
    )
    is_root = position == root
    grad_keys = key_grads[:local_blocks] + jnp.where(is_root, prompt_sum[0], 0.0)
    grad_values = value_grads[:local_blocks] + jnp.where(is_root, prompt_sum[1], 0.0)
    for distance in range(1, reach + 1):
        start = (1 + distance) * local_blocks
        moved = from_behind(
            (key_grads[start : start + local_blocks], value_grads[start : start + local_blocks]),
            "ctx",
            -distance,
        )
        grad_keys = grad_keys + moved[0]
        grad_values = grad_values + moved[1]
    row_count = local_blocks * block_rows
    return (
        attended.reshape(row_count, query_heads * HEAD_WIDTH),
        grad_query.reshape(row_count, query_heads * HEAD_WIDTH),
        grad_keys.reshape(row_count, kv_heads * HEAD_WIDTH),
        grad_values.reshape(row_count, kv_heads * HEAD_WIDTH),
    )


def solution(mesh):
    in_specs = (
        P(("dp", "ctx"), None),
        P(("dp", "ctx"), None),
        P(("dp", "ctx"), None),
        P(("dp", "ctx"), None),
        P(("dp", "ctx"), None),
        P(("dp", "ctx")),
        P(("dp", "ctx")),
        P("dp"),
        P("dp"),
    )
    out_specs = (
        P(("dp", "ctx"), None),
        P(("dp", "ctx"), None),
        P(("dp", "ctx"), None),
        P(("dp", "ctx"), None),
    )
    return jax.shard_map(body, mesh=mesh, in_specs=in_specs, out_specs=out_specs, check_vma=False)
```

profile of v0, /device:TPU:33, one launch (start us, length us, event | category | flops | bytes accessed | tf_op | source)
XLA Modules:
  0.0 486.1 jit_solution(5433476330048423890)
XLA Ops:
  27.6 8.3 %psum.37 = f32[]{:T(128)} all-reduce(f32[]{:T(128)} %convert_reduce_fusion), channel_id=1, replica_groups=mesh['dp'=4,'ctx'=32] {'dp'}, use_global_device_ids=true, to_apply=%region_4.5 | all-reduce | flops 1 | bytes 8 | tf_op jit(solution)/shard_map/psum | solution.py:83
  42.2 85.0 %all-reduce.7.cloned.1.call-done = (bf16[256,512]{1,0:T(8,128)(2,1)}, bf16[256,512]{1,0:T(8,128)(2,1)}) async-done(((bf16[256,512]{1,0:T(8,128)(2,1)}, bf16[256,512]{1,0:T(8,128)(2,1)}), (bf16[256,512]{1,0:T(8,128)(2,1)}, bf16[256,512]{1,0:T(8,128)(2,1)})) %all-reduce.7.cloned.1.call-update) | async-done | bytes 524304 | tf_op jit(solution)/shard_map/psum | solution.py:13
  140.2 9.7 %collective-permute-done.6 = bf16[256,512]{1,0:T(8,128)(2,1)} collective-permute-done((bf16[256,512]{1,0:T(8,128)(2,1)}, bf16[256,512]{1,0:T(8,128)(2,1)}, u32[]{:S(2)}, u32[]{:S(2)}) %collective-permute-start.6) | collective-permute-done | bytes 262176 | tf_op jit(solution)/shard_map/ppermute | solution.py:18
  153.8 183.8 %while.17 = (s32[]{:T(128)}, f32[12,128,4,128]{3,0,2,1:T(8,128)}, f32[12,128,4,128]{3,0,2,1:T(8,128)}, bf16[2,128,4,8,128]{4,3,2,1,0:T(8,128)(2,1)}, bf16[2,128,...) while((s32[]{:T(128)}, f32[12,128,4,128]{3,0,2,1:T(8,128)}, ...), condition=%wide.region_11.12_spmd.clone, body=%wide.region_7.11_spmd.clone.sunk | while | flops 5850748416 | bytes 284402560 | solution.py:143
  185.0 7.8 %fusion.96 = (f32[4,8,128]{2,1,0:T(8,128)S(1)}, f32[4,7,128,128,8]{3,2,4,1,0:T(8,128)}) fusion(pred[128,7,128]{0,2,1:T(8,128)(4,1)S(1)} %pad_add_fusion.7, bf16[1,128,4,8,128]{4,3,2,1,0:T(8,128)(2,1)S(1)} %constant_dynamic-slice_fusion.8, bf16[7,128,4,128,1]{1,3,0,4,2:T(8,128)(2,1)} %copy.128), kind=kOutput, calls=%fused_computation.10.clone.1 | convolution fusion | flops 950530048 | bytes 16777216 | tf_op jit(solution)/shard_map/while/body/eval_jaxpr/ihgd,sjhd->hgisj/dot_general | solution.py:34
  192.8 8.1 %fusion.97 = f32[4,8,128]{2,1,0:T(8,128)S(1)} fusion(f32[4,7,128,128,8]{3,2,4,1,0:T(8,128)} %get-tuple-element.313, f32[4,8,128]{2,1,0:T(8,128)S(1)} %get-tuple-element.314, pred[128,7,128]{0,2,1:T(8,128)(4,1)S(1)} %pad_add_fusion.7), kind=kLoop, calls=%fused_computation.9.clone.1 | loop fusion | flops 14675968 | bytes 14827520 | tf_op jit(solution)/shard_map/while/body/eval_jaxpr/reduce_sum | solution.py:40
  201.0 8.8 %fusion.98 = bf16[4,8,128,7,128]{2,4,1,3,0:T(8,128)(2,1)S(1)} fusion(f32[4,8,128]{2,1,0:T(8,128)S(1)} %fusion.97, f32[4,8,128]{2,1,0:T(8,128)S(1)} %get-tuple-element.314, f32[4,7,128,128,8]{3,2,4,1,0:T(8,128)} %get-tuple-element.313, pred[128,7,128]{0,2,1:T(8,128)(4,1)S(1)} %pad_add_fusion.7), kind=kLoop, calls=%fused_computation.17.clone.1 | loop fusion | flops 18350080 | bytes 22167552 | tf_op jit(solution)/shard_map/while/body/eval_jaxpr/convert_element_type | solution.py:42
  215.2 7.5 %fusion.101 = bf16[4,8,128,7,128]{2,4,1,3,0:T(8,128)(2,1)} fusion(f32[4,8,128]{2,1,0:T(8,128)S(1)} %bitcast.214, f32[4,8,128]{2,1,0:T(8,128)S(1)} %fusion.97, f32[4,8,128]{2,1,0:T(8,128)S(1)} %get-tuple-element.314, f32[4,7,128,128,8]{3,2,4,1,0:T(8,128)S(1)} %bitcast.204, pred[128,7,128]{0,2,1:T(8,128)(4,1)S(1)} %pad_add_fusion.7, ...), kind=kOutput, calls=%fused_computation.5.clone.1 | convolution fusion | flops 968884224 | bytes 24150016 | tf_op jit(solution)/shard_map/while/body/eval_jaxpr/ihgd,sjhd->hgisj/dot_general | solution.py:57
  222.7 4.5 fusion.102
  227.8 3.8 convolution_bitcast_fusion.4
  267.9 7.8 %fusion.96 = (f32[4,8,128]{2,1,0:T(8,128)S(1)}, f32[4,7,128,128,8]{3,2,4,1,0:T(8,128)}) fusion(pred[128,7,128]{0,2,1:T(8,128)(4,1)S(1)} %pad_add_fusion.7, bf16[1,128,4,8,128]{4,3,2,1,0:T(8,128)(2,1)S(1)} %constant_dynamic-slice_fusion.8, bf16[7,128,4,128,1]{1,3,0,4,2:T(8,128)(2,1)} %copy.128), kind=kOutput, calls=%fused_computation.10.clone.1 | convolution fusion | flops 950530048 | bytes 16777216 | tf_op jit(solution)/shard_map/while/body/eval_jaxpr/ihgd,sjhd->hgisj/dot_general | solution.py:34
  275.7 8.1 %fusion.97 = f32[4,8,128]{2,1,0:T(8,128)S(1)} fusion(f32[4,7,128,128,8]{3,2,4,1,0:T(8,128)} %get-tuple-element.313, f32[4,8,128]{2,1,0:T(8,128)S(1)} %get-tuple-element.314, pred[128,7,128]{0,2,1:T(8,128)(4,1)S(1)} %pad_add_fusion.7), kind=kLoop, calls=%fused_computation.9.clone.1 | loop fusion | flops 14675968 | bytes 14827520 | tf_op jit(solution)/shard_map/while/body/eval_jaxpr/reduce_sum | solution.py:40
  283.9 8.8 %fusion.98 = bf16[4,8,128,7,128]{2,4,1,3,0:T(8,128)(2,1)S(1)} fusion(f32[4,8,128]{2,1,0:T(8,128)S(1)} %fusion.97, f32[4,8,128]{2,1,0:T(8,128)S(1)} %get-tuple-element.314, f32[4,7,128,128,8]{3,2,4,1,0:T(8,128)} %get-tuple-element.313, pred[128,7,128]{0,2,1:T(8,128)(4,1)S(1)} %pad_add_fusion.7), kind=kLoop, calls=%fused_computation.17.clone.1 | loop fusion | flops 18350080 | bytes 22167552 | tf_op jit(solution)/shard_map/while/body/eval_jaxpr/convert_element_type | solution.py:42
  298.1 7.5 %fusion.101 = bf16[4,8,128,7,128]{2,4,1,3,0:T(8,128)(2,1)} fusion(f32[4,8,128]{2,1,0:T(8,128)S(1)} %bitcast.214, f32[4,8,128]{2,1,0:T(8,128)S(1)} %fusion.97, f32[4,8,128]{2,1,0:T(8,128)S(1)} %get-tuple-element.314, f32[4,7,128,128,8]{3,2,4,1,0:T(8,128)S(1)} %bitcast.204, pred[128,7,128]{0,2,1:T(8,128)(4,1)S(1)} %pad_add_fusion.7, ...), kind=kOutput, calls=%fused_computation.5.clone.1 | convolution fusion | flops 968884224 | bytes 24150016 | tf_op jit(solution)/shard_map/while/body/eval_jaxpr/ihgd,sjhd->hgisj/dot_general | solution.py:57
  305.6 4.5 fusion.102
  310.7 3.8 convolution_bitcast_fusion.4
  326.8 5.5 %select_add_fusion.5 = f32[12,128,4,128]{3,0,2,1:T(8,128)} fusion(f32[12,128,4,128]{3,0,2,1:T(8,128)} %get-tuple-element.338, f32[7,128,4,128]{3,0,2,1:T(8,128)S(1)} %copy-done.1, pred[]{:T(512)S(6)} %compare.9, s32[7]{0:T(128)S(1)} %pad_add_fusion.8, pred[7]{0:T(512)(128)(4,1)S(1)} %get-tuple-element.316), kind=kOutput, calls=%fused_computation.15.clone.1 | convolution fusion | flops 67633320 | bytes 8126500 | tf_op jit(solution)/shard_map/while/body/eval_jaxpr/sp,sjhd->pjhd/dot_general | solution.py:128
  337.6 6.7 %fusion.48 = (f32[2,128,4,128]{3,0,2,1:T(2,128)}, f32[2,128,4,128]{3,0,2,1:T(2,128)}, f32[2,128,4,128]{3,0,2,1:T(2,128)}, f32[2,128,4,128]{3,0,2,1:T(2,128)}, f32[2,128,4,128]{3,0,2,1:T(2,128)}) fusion(f32[12,128,4,128]{3,0,2,1:T(8,128)} %get-tuple-element.81), kind=kLoop, calls=%fused_computation.108 | loop fusion | bytes 5242880 | tf_op jit(solution)/shard_map/slice | solution.py:147
  344.6 7.0 %collective-permute-start.10 = (f32[2,128,4,128]{3,0,2,1:T(2,128)}, f32[2,128,4,128]{3,0,2,1:T(2,128)}, u32[]{:S(2)}, u32[]{:S(2)}) collective-permute-start(f32[2,128,4,128]{3,0,2,1:T(2,128)} %get-tuple-element.207), channel_id=1, source_target_pairs={{0,29},{1,30},{2,31},{3,0},{4,1},{5,2},{6,3},{7,4},{8,5},{9,6},{10... | collective-permute-start | bytes 1572872 | tf_op jit(solution)/shard_map/ppermute | solution.py:18
  353.7 4.8 collective-permute-done.9
  361.6 7.9 %collective-permute-done.8 = f32[2,128,4,128]{3,0,2,1:T(2,128)} collective-permute-done((f32[2,128,4,128]{3,0,2,1:T(2,128)}, f32[2,128,4,128]{3,0,2,1:T(2,128)}, u32[]{:S(2)}, u32[]{:S(2)}) %collective-permute-start.8) | collective-permute-done | bytes 524320 | tf_op jit(solution)/shard_map/ppermute | solution.py:18
  370.5 16.2 %collective-permute-start.14 = (f32[2,128,4,128]{3,0,2,1:T(2,128)S(1)}, f32[2,128,4,128]{3,0,2,1:T(2,128)}, u32[]{:S(2)}, u32[]{:S(2)}) collective-permute-start(f32[2,128,4,128]{3,0,2,1:T(2,128)S(1)} %get-tuple-element.202), channel_id=1, source_target_pairs={{0,29},{1,30},{2,31},{3,0},{4,1},{5,2},{6,3},{7,4},{8,5},{9,6},{10... | collective-permute-start | bytes 1572872 | tf_op jit(solution)/shard_map/ppermute | solution.py:18
  389.0 4.2 reshape.307
  393.2 78.3 %all-reduce.5.cloned.1.call-done = (f32[2,128,4,128]{3,0,2,1:T(2,128)}, f32[2,128,4,128]{3,0,2,1:T(2,128)}) async-done(((f32[2,128,4,128]{3,0,2,1:T(2,128)}, f32[2,128,4,128]{3,0,2,1:T(2,128)}), (f32[2,128,4,128]{3,0,2,1:T(2,128)}, f32[2,128,4,128]{3,0,2,1:T(2,128)})) %all-reduce.5.cloned.1.call-update) | async-done | bytes 1048592 | tf_op jit(solution)/shard_map/psum | solution.py:146
  (182 shorter events, 135.5 us)
Async XLA Ops:
  7.2 120.0 %all-reduce.7.cloned.1.call-start = ((), (), s32[]{:S(2)}) async-start(), calls=%async_computation.1 | async-start | bytes 1048576 | tf_op jit(solution)/shard_map/psum | solution.py:13
  7.2 124.3 %collective-permute-start.1 = (bf16[256,512]{1,0:T(8,128)(2,1)}, bf16[256,512]{1,0:T(8,128)(2,1)}, u32[]{:S(2)}, u32[]{:S(2)}) collective-permute-start(bf16[256,512]{1,0:T(8,128)(2,1)} %param.12), channel_id=1, source_target_pairs={{0,2},{1,3},{2,4},{3,5},{4,6},{5,7},{6,8},{7,9},{8,10},{9,11},{10,... | collective-permute-start | bytes 786440 | tf_op jit(solution)/shard_map/ppermute | solution.py:18
  8.5 120.6 %collective-permute-start = (bf16[256,512]{1,0:T(8,128)(2,1)}, bf16[256,512]{1,0:T(8,128)(2,1)}, u32[]{:S(2)}, u32[]{:S(2)}) collective-permute-start(bf16[256,512]{1,0:T(8,128)(2,1)} %param.12), channel_id=1, source_target_pairs={{0,1},{1,2},{2,3},{3,4},{4,5},{5,6},{6,7},{7,8},{8,9},{9,10},{10,1... | collective-permute-start | bytes 786440 | tf_op jit(solution)/shard_map/ppermute | solution.py:18
  10.5 123.5 %collective-permute-start.2 = (bf16[256,512]{1,0:T(8,128)(2,1)}, bf16[256,512]{1,0:T(8,128)(2,1)}, u32[]{:S(2)}, u32[]{:S(2)}) collective-permute-start(bf16[256,512]{1,0:T(8,128)(2,1)} %param.12), channel_id=1, source_target_pairs={{0,3},{1,4},{2,5},{3,6},{4,7},{5,8},{6,9},{7,10},{8,11},{9,12},{10... | collective-permute-start | bytes 786440 | tf_op jit(solution)/shard_map/ppermute | solution.py:18
  11.8 125.5 %collective-permute-start.3 = (bf16[256,512]{1,0:T(8,128)(2,1)}, bf16[256,512]{1,0:T(8,128)(2,1)}, u32[]{:S(2)}, u32[]{:S(2)}) collective-permute-start(bf16[256,512]{1,0:T(8,128)(2,1)} %param.12), channel_id=1, source_target_pairs={{0,4},{1,5},{2,6},{3,7},{4,8},{5,9},{6,10},{7,11},{8,12},{9,13},{1... | collective-permute-start | bytes 786440 | tf_op jit(solution)/shard_map/ppermute | solution.py:18
  13.3 126.9 %collective-permute-start.5 = (bf16[256,512]{1,0:T(8,128)(2,1)}, bf16[256,512]{1,0:T(8,128)(2,1)S(1)}, u32[]{:S(2)}, u32[]{:S(2)}) collective-permute-start(bf16[256,512]{1,0:T(8,128)(2,1)} %param.13), channel_id=1, source_target_pairs={{0,2},{1,3},{2,4},{3,5},{4,6},{5,7},{6,8},{7,9},{8,10},{9,11},{10,... | collective-permute-start | bytes 786440 | tf_op jit(solution)/shard_map/ppermute | solution.py:18
  21.8 449.7 %all-reduce.5.cloned.1.call-start = ((), (), s32[]{:S(2)}) async-start(), calls=%async_computation | async-start | bytes 2097152 | tf_op jit(solution)/shard_map/psum | solution.py:146
  129.1 9.2 %collective-permute-start.4 = (bf16[256,512]{1,0:T(8,128)(2,1)}, bf16[256,512]{1,0:T(8,128)(2,1)S(1)}, u32[]{:S(2)}, u32[]{:S(2)}) collective-permute-start(bf16[256,512]{1,0:T(8,128)(2,1)} %param.13), channel_id=1, source_target_pairs={{0,1},{1,2},{2,3},{3,4},{4,5},{5,6},{6,7},{7,8},{8,9},{9,10},{10,1... | collective-permute-start | bytes 786440 | tf_op jit(solution)/shard_map/ppermute | solution.py:18
  131.5 18.5 %collective-permute-start.6 = (bf16[256,512]{1,0:T(8,128)(2,1)}, bf16[256,512]{1,0:T(8,128)(2,1)}, u32[]{:S(2)}, u32[]{:S(2)}) collective-permute-start(bf16[256,512]{1,0:T(8,128)(2,1)} %param.13), channel_id=1, source_target_pairs={{0,3},{1,4},{2,5},{3,6},{4,7},{5,8},{6,9},{7,10},{8,11},{9,12},{10... | collective-permute-start | bytes 786440 | tf_op jit(solution)/shard_map/ppermute | solution.py:18
  134.0 16.9 %collective-permute-start.7 = (bf16[256,512]{1,0:T(8,128)(2,1)}, bf16[256,512]{1,0:T(8,128)(2,1)}, u32[]{:S(2)}, u32[]{:S(2)}) collective-permute-start(bf16[256,512]{1,0:T(8,128)(2,1)} %param.13), channel_id=1, source_target_pairs={{0,4},{1,5},{2,6},{3,7},{4,8},{5,9},{6,10},{7,11},{8,12},{9,13},{1... | collective-permute-start | bytes 786440 | tf_op jit(solution)/shard_map/ppermute | solution.py:18
  138.3 15.5 %copy-start.10 = (s32[256]{0:T(256)S(1)}, s32[256]{0:T(256)}, u32[]{:S(2)}) copy-start(s32[256]{0:T(256)} %param.16) | copy-start | bytes 3076
  201.0 14.2 %slice-start = ((s8[14680064]{0:T(1024)(128)(4,1)}), s8[4194304]{0:T(1024)(128)(4,1)S(1)}, s32[]{:S(2)}) async-start(s8[14680064]{0:T(1024)(128)(4,1)} %bitcast.203), calls=%async_computation.2 | async-start | bytes 8388608 | tf_op jit(solution)/shard_map/while
  201.0 14.2 %slice-start.1 = ((s8[14680064]{0:T(1024)(128)(4,1)}), s8[4194304]{0:T(1024)(128)(4,1)S(1)}, s32[]{:S(2)}) async-start(s8[14680064]{0:T(1024)(128)(4,1)} %bitcast.203), calls=%async_computation.3 | async-start | bytes 8388608 | tf_op jit(solution)/shard_map/while
  283.8 14.2 %slice-start = ((s8[14680064]{0:T(1024)(128)(4,1)}), s8[4194304]{0:T(1024)(128)(4,1)S(1)}, s32[]{:S(2)}) async-start(s8[14680064]{0:T(1024)(128)(4,1)} %bitcast.203), calls=%async_computation.2 | async-start | bytes 8388608 | tf_op jit(solution)/shard_map/while
  283.8 14.2 %slice-start.1 = ((s8[14680064]{0:T(1024)(128)(4,1)}), s8[4194304]{0:T(1024)(128)(4,1)S(1)}, s32[]{:S(2)}) async-start(s8[14680064]{0:T(1024)(128)(4,1)} %bitcast.203), calls=%async_computation.3 | async-start | bytes 8388608 | tf_op jit(solution)/shard_map/while
  344.3 42.4 %copy-start.8 = (bf16[2,128,4,8,128]{4,3,2,1,0:T(8,128)(2,1)S(1)}, bf16[2,128,4,8,128]{4,3,2,1,0:T(8,128)(2,1)}, u32[]{:S(2)}) copy-start(bf16[2,128,4,8,128]{4,3,2,1,0:T(8,128)(2,1)} %get-tuple-element.80) | copy-start | bytes 6291460
  344.3 14.2 %collective-permute-start.9 = (f32[2,128,4,128]{3,0,2,1:T(2,128)}, f32[2,128,4,128]{3,0,2,1:T(2,128)}, u32[]{:S(2)}, u32[]{:S(2)}) collective-permute-start(f32[2,128,4,128]{3,0,2,1:T(2,128)} %get-tuple-element.204), channel_id=1, source_target_pairs={{0,30},{1,31},{2,0},{3,1},{4,2},{5,3},{6,4},{7,5},{8,6},{9,7},{10,... | collective-permute-start | bytes 1572872 | tf_op jit(solution)/shard_map/ppermute | solution.py:18
  344.3 25.1 %collective-permute-start.8 = (f32[2,128,4,128]{3,0,2,1:T(2,128)}, f32[2,128,4,128]{3,0,2,1:T(2,128)}, u32[]{:S(2)}, u32[]{:S(2)}) collective-permute-start(f32[2,128,4,128]{3,0,2,1:T(2,128)} %get-tuple-element.205), channel_id=1, source_target_pairs={{0,31},{1,0},{2,1},{3,2},{4,3},{5,4},{6,5},{7,6},{8,7},{9,8},{10,9... | collective-permute-start | bytes 1572872 | tf_op jit(solution)/shard_map/ppermute | solution.py:18
  344.6 25.9 %collective-permute-start.11 = (f32[2,128,4,128]{3,0,2,1:T(2,128)}, f32[2,128,4,128]{3,0,2,1:T(2,128)}, u32[]{:S(2)}, u32[]{:S(2)}) collective-permute-start(f32[2,128,4,128]{3,0,2,1:T(2,128)} %get-tuple-element.206), channel_id=1, source_target_pairs={{0,28},{1,29},{2,30},{3,31},{4,0},{5,1},{6,2},{7,3},{8,4},{9,5},{1... | collective-permute-start | bytes 1572872 | tf_op jit(solution)/shard_map/ppermute | solution.py:18
  344.6 48.6 %collective-permute-start.10 = (f32[2,128,4,128]{3,0,2,1:T(2,128)}, f32[2,128,4,128]{3,0,2,1:T(2,128)}, u32[]{:S(2)}, u32[]{:S(2)}) collective-permute-start(f32[2,128,4,128]{3,0,2,1:T(2,128)} %get-tuple-element.207), channel_id=1, source_target_pairs={{0,29},{1,30},{2,31},{3,0},{4,1},{5,2},{6,3},{7,4},{8,5},{9,6},{10... | collective-permute-start | bytes 1572872 | tf_op jit(solution)/shard_map/ppermute | solution.py:18
  353.6 121.0 %collective-permute-start.12 = (f32[2,128,4,128]{3,0,2,1:T(2,128)}, f32[2,128,4,128]{3,0,2,1:T(2,128)}, u32[]{:S(2)}, u32[]{:S(2)}) collective-permute-start(f32[2,128,4,128]{3,0,2,1:T(2,128)} %get-tuple-element.198), channel_id=1, source_target_pairs={{0,31},{1,0},{2,1},{3,2},{4,3},{5,4},{6,5},{7,6},{8,7},{9,8},{10,9... | collective-permute-start | bytes 1572872 | tf_op jit(solution)/shard_map/ppermute | solution.py:18
  358.6 116.1 %collective-permute-start.13 = (f32[2,128,4,128]{3,0,2,1:T(2,128)}, f32[2,128,4,128]{3,0,2,1:T(2,128)}, u32[]{:S(2)}, u32[]{:S(2)}) collective-permute-start(f32[2,128,4,128]{3,0,2,1:T(2,128)} %get-tuple-element.199), channel_id=1, source_target_pairs={{0,30},{1,31},{2,0},{3,1},{4,2},{5,3},{6,4},{7,5},{8,6},{9,7},{10,... | collective-permute-start | bytes 1572872 | tf_op jit(solution)/shard_map/ppermute | solution.py:18
  369.4 105.2 %collective-permute-start.15 = (f32[2,128,4,128]{3,0,2,1:T(2,128)S(1)}, f32[2,128,4,128]{3,0,2,1:T(2,128)}, u32[]{:S(2)}, u32[]{:S(2)}) collective-permute-start(f32[2,128,4,128]{3,0,2,1:T(2,128)S(1)} %get-tuple-element.201), channel_id=1, source_target_pairs={{0,28},{1,29},{2,30},{3,31},{4,0},{5,1},{6,2},{7,3},{8,4},{9,5},{1... | collective-permute-start | bytes 1572872 | tf_op jit(solution)/shard_map/ppermute | solution.py:18
  370.5 104.1 %collective-permute-start.14 = (f32[2,128,4,128]{3,0,2,1:T(2,128)S(1)}, f32[2,128,4,128]{3,0,2,1:T(2,128)}, u32[]{:S(2)}, u32[]{:S(2)}) collective-permute-start(f32[2,128,4,128]{3,0,2,1:T(2,128)S(1)} %get-tuple-element.202), channel_id=1, source_target_pairs={{0,29},{1,30},{2,31},{3,0},{4,1},{5,2},{6,3},{7,4},{8,5},{9,6},{10... | collective-permute-start | bytes 1572872 | tf_op jit(solution)/shard_map/ppermute | solution.py:18
  (20 other events, 105.8 us)
Sparse Core Ops, SparseCore 0:
  21.9 105.2 all-reduce.6
  353.7 117.7 all-reduce.4
where the time goes:
time: 492 us; the launch traced here: 486 us
  waiting for transfers between devices  186 us (38%)
  local copies, waits for them, and re-layouts  88 us (18%)
  matrix products  73.1 us (15%)
  other arithmetic  54.6 us (11%)
  starting transfers between devices  40.3 us (8%)
  between operations  19.3 us (4%)
  loops' own time  16.7 us (3%)
  blocking collectives  8.32 us (2%)
    psum x1, waiting for transfers between devices, from_root(): return lax.psum(jnp.where(mine, array, jnp.zeros_like(array)), axis)  85 us
    psum x1, waiting for transfers between devices, body(): lax.psum((key_grads[local_blocks:2 * local_blocks], value_grads[local_blo...  78.3 us
    ppermute x16, starting transfers between devices, from_behind(): lax.ppermute(array, axis, [(i, (i + by) % size) for i in range(size)])  40.2 us
    ppermute x16, waiting for transfers between devices, from_behind(): lax.ppermute(array, axis, [(i, (i + by) % size) for i in range(size)])  22.5 us
    convert_element_type x2, other arithmetic, block_step(): prob_low = probability.astype(jnp.bfloat16)  17.5 us
    another operation x1, loops' own time, body(): lax.scan(visit, (zero_filled, zero_filled), inputs)  16.7 us
    reduce_sum x2, other arithmetic, block_step(): denominator = jnp.sum(exponent, axis=(3, 4), keepdims=True)  16.2 us
    dot_general x2, matrix products, block_step(): jnp.einsum('ihgd,sjhd->hgisj', query_block, slot_keys, preferred_element_...  15.6 us
  transfers between devices with their start and end apart: 18, of which 5 were waited for; matrix products, arithmetic and copies ran while one was open for 7% of the time, Pallas kernels for 0%

commit v1 on v0

v1 whole, which is shorter than its diff:
```python
import functools
import math

import jax
import jax.numpy as jnp
from jax import lax
from jax.experimental import pallas as pl
from jax.experimental.pallas import tpu as pltpu
from jax.sharding import PartitionSpec as P

MESH = pl.DeviceIdType.MESH
F32, BF16 = jnp.float32, jnp.bfloat16
W = 128
T = 2 * W
R = 8
C = R * W
N = 7 * W
HOPS = 4
K_, V_ = 0, 1


def nn(a, b):
    return lax.dot_general(a, b, (((1,), (0,)), ((), ())), preferred_element_type=F32)


def nt(a, b):
    return lax.dot_general(a, b, (((1,), (1,)), ((), ())), preferred_element_type=F32)


def tn(a, b):
    return lax.dot_general(a, b, (((0,), (0,)), ((), ())), preferred_element_type=F32)


SCRATCH = dict(
    kvp=pltpu.VMEM((2, 2, 6, T, W), BF16),
    qb=pltpu.VMEM((2, 2, T, C), BF16),
    ub=pltpu.VMEM((2, 2, T, C), BF16),
    ob=pltpu.VMEM((2, 2, T, C), BF16),
    gb=pltpu.VMEM((2, 2, T, C), BF16),
    cand=pltpu.VMEM((16, 2, 2, 16, W), BF16),
    scat=pltpu.VMEM((16, 2, 2, 16, W), BF16),
    sel=pltpu.VMEM((2, 2, 16, W), BF16),
    gath=pltpu.VMEM((16, 2, 2, 16, W), BF16),
    meta=pltpu.VMEM((2, 2, 8, W), jnp.int32),
    lens=pltpu.VMEM((4, 8, W), jnp.int32),
    wt=pltpu.VMEM((2, 2, W, W), F32),
    mb=pltpu.VMEM((2, 2, W, W), F32),
    ku=pltpu.VMEM((4, N, W), BF16),
    vu=pltpu.VMEM((4, N, W), BF16),
    pf=pltpu.VMEM((4, 4, N, 2 * W), F32),
    dl=pltpu.VMEM((4, 4, 8, 2 * W), F32),
    do=pltpu.VMEM((4, 4, 2 * W, W), BF16),
    ps=pltpu.VMEM((N, 2 * W), F32),
    acc=pltpu.VMEM((N, W), F32),
    gacc=pltpu.VMEM((6, T, W), F32),
    pacc=pltpu.VMEM((T, W), F32),
    own=pltpu.VMEM((2, 2, T, W), F32),
    msend=pltpu.VMEM((2, 2, T, W), F32),
    mrecv=pltpu.VMEM((2, 2, T, W), F32),
    gsend=pltpu.VMEM((2, 2, 4, T, W), BF16),
    grecv=pltpu.VMEM((2, 2, 2, 2, T, W), BF16),
    psend=pltpu.VMEM((2, 2, 16, 16, W), BF16),
    prec=pltpu.VMEM((2, 2, 16, 16, W), BF16),
    agsend=pltpu.VMEM((2, 2, 16, W), BF16),
    ag=pltpu.VMEM((2, 32, 2, 16, W), BF16),
    one_send=pltpu.SemaphoreType.DMA((64,)),
    local=pltpu.SemaphoreType.DMA((12,)),
    kv_recv=pltpu.SemaphoreType.DMA((2, 2)),
    mate_kv=pltpu.SemaphoreType.DMA,
    meta_recv=pltpu.SemaphoreType.DMA,
    lens_send=pltpu.SemaphoreType.DMA,
    lens_recv=pltpu.SemaphoreType.DMA,
    qu_recv=pltpu.SemaphoreType.DMA((2, 2)),
    out_recv=pltpu.SemaphoreType.DMA((2, 2)),
    pr_send=pltpu.SemaphoreType.DMA((2,)),
    pr_recv=pltpu.SemaphoreType.DMA((2,)),
    g_recv=pltpu.SemaphoreType.DMA((2, 2)),
    m_recv=pltpu.SemaphoreType.DMA((2, 2)),
    ps_send=pltpu.SemaphoreType.DMA((2, 2)),
    ps_recv=pltpu.SemaphoreType.DMA((2, 2)),
    ag_send=pltpu.SemaphoreType.DMA((2,)),
    ag_recv=pltpu.SemaphoreType.DMA((2,)),
)


class Names:
    def __init__(self, names, refs):
        for name, ref in zip(names, refs):
            setattr(self, name, ref)


def kernel(groups, ring, q, k, v, u, anc, seg, resp, rew, leng, attn, gq, gk, gv, *refs):
    s = Names(list(SCRATCH), refs)
    me, z = lax.axis_index("ctx"), lax.axis_index("dp")
    chips = ring // 2
    chip, core = me // 2, lax.rem(me, 2)
    other = 1 - core
    mate = 2 * chip + other
    inv_root = 1.0 / math.sqrt(W)
    exp_scale = math.log2(math.e) * inv_root

    first = anc[0, 0]
    root = jnp.where(first < 0, me, lax.div(first, 2))
    root_chip, root_core = lax.div(root, 2), lax.rem(root, 2)

    sends = []

    def send(src, dst, recv_sem, to):
        copy = pltpu.make_async_remote_copy(
            src_ref=src,
            dst_ref=dst,
            send_sem=s.one_send.at[len(sends)],
            recv_sem=recv_sem,
            device_id={"ctx": to},
            device_id_type=MESH,
        )
        copy.start()
        sends.append(copy)

    def await_bytes(ref, sem):
        pltpu.make_async_copy(ref, ref, sem).wait()

    barrier = pltpu.get_barrier_semaphore()

    def greet(i, carry):
        pl.semaphore_signal(
            barrier, inc=1, device_id={"ctx": lax.rem(me + i, ring)}, device_id_type=MESH
        )
        return carry

    lax.fori_loop(1, ring, greet, 0)
    for i in range(1, groups):
        pl.semaphore_signal(
            barrier, inc=1, device_id={"dp": lax.rem(z + i, groups)}, device_id_type=MESH
        )

    def kcols(lane, h):
        return pl.ds(pl.multiple_of((2 * lane + h) * W, W), W)

    def qcols(lane, h):
        return pl.ds(pl.multiple_of((2 * lane + h) * C, C), C)

    local = []

    def fetch(src, dst):
        copy = pltpu.make_async_copy(src, dst, s.local.at[len(local)])
        copy.start()
        local.append(copy)
        return copy

    own_kv = [
        fetch(src.at[:, kcols(core, h)], s.kvp.at[kv, h, 4 + core])
        for h in range(2)
        for kv, src in ((K_, k), (V_, v))
    ]
    own_qu = [
        (
            fetch(q.at[:, qcols(core, h)], s.qb.at[core, h]),
            fetch(u.at[:, qcols(core, h)], s.ub.at[core, h]),
        )
        for h in range(2)
    ]

    total = leng[0]
    for i in range(1, 16):
        total = total + leng[i]
    s.lens[z] = jnp.full((8, W), total, jnp.int32)
    for b in range(2):
        rows = [jnp.where(anc[b, 0] >= 0, 1, 0), jnp.where(anc[b, 1] >= 0, 1, 0)]
        for hop in range(1, HOPS + 1):
            chosen = jnp.int32(-1)
            for slot in range(2, 6):
                a = anc[b, slot]
                away = lax.rem(me - lax.div(jnp.maximum(a, 0), 2) + ring, ring)
                chosen = jnp.where((a >= 0) & (away == hop), lax.rem(a, 2), chosen)
            rows.append(chosen)
        for i, row in enumerate(rows):
            s.meta[core, b, i : i + 1, :] = jnp.full((1, W), row, jnp.int32)
        s.meta[core, b, 6:7, :] = seg[b : b + 1, :]
        s.meta[core, b, 7:8, :] = resp[b : b + 1, :]

    pl.semaphore_wait(barrier, ring - 1 + groups - 1)

    for h in range(2):
        for kv, src in ((K_, k), (V_, v)):
            send(src.at[:, kcols(other, h)], s.kvp.at[kv, h, 4 + core], s.mate_kv, mate)
    for i in range(1, groups):
        pltpu.make_async_remote_copy(
            src_ref=s.lens.at[z],
            dst_ref=s.lens.at[z],
            send_sem=s.lens_send,
            recv_sem=s.lens_recv,
            device_id={"dp": lax.rem(z + i, groups)},
            device_id_type=MESH,
        ).start()
    send(s.meta.at[core], s.meta.at[core], s.meta_recv, mate)

    def send_chain(h):
        for kv, src in ((K_, k), (V_, v)):
            for hop in (1, 2):
                for lane in range(2):
                    send(
                        src.at[:, kcols(lane, h)],
                        s.kvp.at[kv, h, 2 * (2 - hop) + core],
                        s.kv_recv.at[kv, h],
                        2 * lax.rem(chip + hop, chips) + lane,
                    )

    def send_qu(h):
        send(q.at[:, qcols(other, h)], s.qb.at[core, h], s.qu_recv.at[h, 0], mate)
        send(u.at[:, qcols(other, h)], s.ub.at[core, h], s.qu_recv.at[h, 1], mate)

    send_chain(0)
    send_qu(0)

    for copy in own_kv:
        copy.wait()
    await_bytes(s.kvp.at[0, 0, pl.ds(0, 4)], s.mate_kv)
    for h in range(2):
        for kv in range(2):
            x = lax.select(root_core == 0, s.kvp[kv, h, 4], s.kvp[kv, h, 5])
            s.cand[:, h, kv] = x.reshape(16, 16, W)

    def to_chips(start):
        def step(i, carry):
            start(lax.rem(chip + i, chips))
            return carry

        lax.fori_loop(1, chips, step, 0)

    def loop_send(src, dst, send_sem, recv_sem, to):
        pltpu.make_async_remote_copy(
            src_ref=src,
            dst_ref=dst,
            send_sem=send_sem,
            recv_sem=recv_sem,
            device_id={"ctx": to},
            device_id_type=MESH,
        ).start()

    to_chips(
        lambda c: loop_send(
            s.cand.at[c], s.scat.at[chip], s.pr_send.at[0], s.pr_recv.at[0], 2 * c + core
        )
    )
    s.scat[chip] = s.cand[chip]
    send_chain(1)
    send_qu(1)

    await_bytes(s.meta.at[0], s.meta_recv)
    await_bytes(s.lens.at[pl.ds(0, groups - 1)], s.lens_recv)
    everything = s.lens[0, 0:1, :]
    for i in range(1, groups):
        everything = everything + s.lens[i, 0:1, :]
    scale = float(groups * 16 * W) / everything.astype(F32)
    scored = [rew[i].astype(F32) for i in range(16)]
    centre = functools.reduce(lambda a, b: a + b, scored) * (1.0 / 16)
    apart = [x - centre for x in scored]
    variance = functools.reduce(lambda a, b: a + b, [x * x for x in apart]) * (1.0 / 16)
    spread = jnp.sqrt(jnp.full((1, W), variance, F32))
    divisor = jnp.maximum(spread, 0.5)
    key_row = lax.broadcasted_iota(jnp.int32, (W, W), 0)
    query_col = lax.broadcasted_iota(jnp.int32, (W, W), 1)
    for o in range(2):
        for b in range(2):
            answer = s.meta[o, b, 7:8, :]
            row = jnp.zeros((1, W), F32)
            for i in range(16):
                row = row + jnp.where(answer == i, apart[i], 0.0)
            row = row / divisor * scale
            s.wt[o, b] = jnp.transpose(jnp.broadcast_to(row, (W, W)))
            of_query = jnp.broadcast_to(s.meta[o, b, 6:7, :].astype(F32), (W, W))
            of_key = jnp.transpose(of_query)
            seen = (key_row <= query_col) & (of_query >= 0.0)
            seen = seen & ((of_key == of_query) | (of_key == 0.0))
            seen = seen | (key_row == query_col)
            s.mb[o, b] = jnp.where(seen, 0.0, -jnp.inf)

    await_bytes(s.scat.at[pl.ds(0, chips - 1)], s.pr_recv.at[0])
    prompt_slice = s.scat[root_chip]
    s.sel[...] = prompt_slice
    s.gath[chip] = prompt_slice
    to_chips(
        lambda c: loop_send(s.sel, s.gath.at[chip], s.pr_send.at[1], s.pr_recv.at[1], 2 * c + core)
    )

    def where_is(t, h):
        return lax.rem(core + t // 2 + h, 2), lax.rem(t, 2)

    def gather_block(t, h, kv, to):
        o, b = where_is(t, h)
        to[t, 0 : 2 * W] = s.gath[:, h, kv].reshape(T, W)
        for i in range(HOPS):
            chosen = s.meta[o, b, 5 - i : 6 - i, :]
            both = s.kvp[kv, h, o + i].astype(F32)
            picked = jnp.where(jnp.broadcast_to(chosen, (W, W)) == 1, both[W:], both[:W])
            to[t, (2 + i) * W : (3 + i) * W] = picked.astype(BF16)
        to[t, 6 * W :] = s.kvp[kv, h, o + 4, pl.ds(pl.multiple_of(b * W, W), W), :]

    def spread_block(t, h):
        o, b = where_is(t, h)
        s.pacc[...] += s.acc[0 : 2 * W]
        for i in range(HOPS):
            chosen = jnp.broadcast_to(s.meta[o, b, 5 - i : 6 - i, :], (W, W)) == 1
            x = s.acc[(2 + i) * W : (3 + i) * W]
            s.gacc[o + i, 0:W] += jnp.where(chosen, 0.0, x)
            s.gacc[o + i, W:] += jnp.where(chosen, x, 0.0)
        s.gacc[o + 4, pl.ds(pl.multiple_of(b * W, W), W), :] += s.acc[6 * W :]

    def pair(ref, o, h, b, g):
        rows = pl.ds(pl.multiple_of(b * W, W), W)
        return [ref.at[o, h, rows, pl.ds((2 * g + i) * W, W)] for i in range(2)]

    def forward(h):
        def step(t, carry):
            o, b = where_is(t, h)
            gather_block(t, h, K_, s.ku)
            gather_block(t, h, V_, s.vu)
            bias = []
            for i in range(6):
                row = s.meta[o, b, (0, 1, 5, 4, 3, 2)[i] : (0, 1, 5, 4, 3, 2)[i] + 1, :]
                unseen = row <= 0 if i < 2 else row < 0
                row = jnp.where(unseen, -jnp.inf, 0.0)
                bias.append(jnp.concatenate([row, row], axis=1))
            mask = jnp.concatenate([s.mb[o, b], s.mb[o, b]], axis=1)
            weight = s.wt[o, b]
            for g in range(4):
                queries = jnp.concatenate([x[...] for x in pair(s.qb, o, h, b, g)], axis=0)
                scores = nt(s.ku[t], queries)
                s.ps[0 : 6 * W] = scores[0 : 6 * W]
                s.ps[6 * W :] = scores[6 * W :] + mask
                peak = jnp.max(s.ps[6 * W :], axis=0, keepdims=True)
                for i in range(6):
                    top = jnp.max(s.ps[i * W : (i + 1) * W], axis=0, keepdims=True)
                    peak = jnp.maximum(peak, top + bias[i])
                shift = peak * exp_scale
                denominator = jnp.zeros((1, 2 * W), F32)
                for i in range(7):
                    here = shift if i == 6 else shift - bias[i]
                    e = jnp.exp2(s.ps[i * W : (i + 1) * W] * exp_scale - here)
                    s.ps[i * W : (i + 1) * W] = e
                    denominator = denominator + jnp.sum(e, axis=0, keepdims=True)
                probs = s.ps[...] * (1.0 / denominator)
                s.pf[t, g] = probs
                low = probs.astype(BF16)
                up = [x[...].astype(F32) * weight for x in pair(s.ub, o, h, b, g)]
                grad_out = jnp.concatenate(up, axis=0).astype(BF16)
                s.do[t, g] = grad_out
                attended = jnp.transpose(tn(s.vu[t], low)).astype(BF16)
                for i, x in enumerate(pair(s.ob, o, h, b, g)):
                    x[...] = attended[i * W : (i + 1) * W]
                product = grad_out.astype(F32) * attended.astype(F32)
                s.dl[t, g, 0:1] = jnp.sum(jnp.transpose(product), axis=0, keepdims=True)
                term = nn(low, grad_out)
                if g == 0:
                    s.acc[...] = term
                else:
                    s.acc[...] += term
            spread_block(t, h)
            return carry

        lax.fori_loop(0, 4, step, 0)

    def backward(h):
        def step(t, carry):
            o, b = where_is(t, h)
            for g in range(4):
                queries = jnp.concatenate([x[...] for x in pair(s.qb, o, h, b, g)], axis=0)
                dprobs = nt(s.vu[t], s.do[t, g])
                dscores = s.pf[t, g] * (dprobs - s.dl[t, g, 0:1]) * inv_root
                dscores = dscores.astype(BF16)
                grad = jnp.transpose(tn(s.ku[t], dscores)).astype(BF16)
                for i, x in enumerate(pair(s.gb, o, h, b, g)):
                    x[...] = grad[i * W : (i + 1) * W]
                term = nn(dscores, queries)
                if g == 0:
                    s.acc[...] = term
                else:
                    s.acc[...] += term
            spread_block(t, h)
            return carry

        lax.fori_loop(0, 4, step, 0)

    def clear():
        s.gacc[...] = jnp.zeros_like(s.gacc)
        s.pacc[...] = jnp.zeros_like(s.pacc)

    def send_grads(kv, h):
        for i in range(4):
            s.gsend[kv, h, i] = s.gacc[i].astype(BF16)
            hop = 2 if i < 2 else 1
            send(
                s.gsend.at[kv, h, i],
                s.grecv.at[kv, h, hop - 1, core],
                s.g_recv.at[kv, h],
                2 * lax.rem(chip - hop + chips, chips) + i % 2,
            )
        s.psend[kv, h] = s.pacc[...].reshape(16, 16, W).astype(BF16)
        to_chips(
            lambda c: loop_send(
                s.psend.at[kv, h, c],
                s.prec.at[kv, h, chip],
                s.ps_send.at[kv, h],
                s.ps_recv.at[kv, h],
                2 * c + core,
            )
        )
        s.prec[kv, h, chip] = s.psend[kv, h, chip]
        s.msend[kv, h] = s.gacc[4 + other]
        send(s.msend.at[kv, h], s.mrecv.at[kv, h], s.m_recv.at[kv, h], mate)
        s.own[kv, h] = s.gacc[4 + core]

    own_out = []

    def send_rows(staged, out, h, recv_sem):
        send(staged.at[other, h], out.at[:, qcols(core, h)], recv_sem, mate)
        own_out.append(fetch(staged.at[core, h], out.at[:, qcols(core, h)]))

    def sum_prompt(h):
        for kv in range(2):
            await_bytes(s.prec.at[kv, h, pl.ds(0, chips - 1)], s.ps_recv.at[kv, h])
            summed = jnp.sum(s.prec[kv, h].astype(F32), axis=0).astype(BF16)
            s.agsend[h, kv] = summed
            s.ag[h, 16 * core + chip, kv] = summed

        def step(i, carry):
            loop_send(
                s.agsend.at[h],
                s.ag.at[h, 16 * core + chip],
                s.ag_send.at[h],
                s.ag_recv.at[h],
                lax.rem(me + i, ring),
            )
            return carry

        lax.fori_loop(1, ring, step, 0)

    def finish(h):
        await_bytes(s.ag.at[h, pl.ds(0, ring - 1)], s.ag_recv.at[h])
        for kv, out in ((K_, gk), (V_, gv)):
            await_bytes(s.grecv.at[kv, h], s.g_recv.at[kv, h])
            await_bytes(s.mrecv.at[kv, h], s.m_recv.at[kv, h])
            for lane, mine in ((core, s.own), (other, s.mrecv)):
                x = mine[kv, h] + s.grecv[kv, h, 0, lane].astype(F32)
                x = x + s.grecv[kv, h, 1, lane].astype(F32)
                prompt = s.ag[h, pl.ds(16 * lane, 16), kv].astype(F32).reshape(T, W)
                here = jnp.full((T, W), root, jnp.int32) == me
                out[:, kcols(lane, h)] = x + jnp.where(here, prompt, 0.0)

    for h in range(2):
        if h == 0:
            await_bytes(s.gath.at[pl.ds(0, chips - 1)], s.pr_recv.at[1])
        for kv in range(2):
            await_bytes(s.kvp.at[kv, h, pl.ds(0, 4)], s.kv_recv.at[kv, h])
            await_bytes((s.qb, s.ub)[kv].at[other, h], s.qu_recv.at[h, kv])
            own_qu[h][kv].wait()
        clear()
        forward(h)
        send_grads(V_, h)
        send_rows(s.ob, attn, h, s.out_recv.at[0, h])
        if h == 1:
            sum_prompt(0)
        clear()
        backward(h)
        send_grads(K_, h)
        send_rows(s.gb, gq, h, s.out_recv.at[1, h])
    finish(0)
    sum_prompt(1)
    finish(1)

    for copy in own_out:
        copy.wait()
    for h in range(2):
        for i in range(2):
            await_bytes(s.ob.at[other, h], s.out_recv.at[i, h])
    for copy in sends:
        copy.wait_send()
    await_bytes(s.lens.at[pl.ds(0, groups - 1)], s.lens_send)
    for i in range(2):
        await_bytes(s.scat.at[pl.ds(0, chips - 1)], s.pr_send.at[i])
        await_bytes(s.ag.at[i, pl.ds(0, ring - 1)], s.ag_send.at[i])
        for h in range(2):
            await_bytes(s.prec.at[i, h, pl.ds(0, chips - 1)], s.ps_send.at[i, h])


def body(queries, keys, values, upstream, ancestors, segments, responses, rewards, lengths):
    any_spec = pl.BlockSpec(memory_space=pl.ANY)
    smem = pl.BlockSpec(memory_space=pltpu.SMEM)
    vmem = pl.BlockSpec(memory_space=pltpu.VMEM)
    return pl.pallas_call(
        functools.partial(kernel, lax.axis_size("dp"), lax.axis_size("ctx")),
        out_shape=[
            jax.ShapeDtypeStruct(queries.shape, BF16),
            jax.ShapeDtypeStruct(queries.shape, BF16),
            jax.ShapeDtypeStruct(keys.shape, F32),
            jax.ShapeDtypeStruct(keys.shape, F32),
        ],
        in_specs=[any_spec] * 4 + [smem, vmem, vmem, smem, smem],
        out_specs=[vmem] * 4,
        scratch_shapes=list(SCRATCH.values()),
        compiler_params=pltpu.CompilerParams(
            collective_id=0, has_side_effects=True, vmem_limit_bytes=60 * 1024 * 1024
        ),
    )(
        queries,
        keys,
        values,
        upstream,
        ancestors,
        segments.reshape(2, W),
        responses.reshape(2, W),
        rewards,
        lengths,
    )


def solution(mesh):
    rows, flat = P(("dp", "ctx"), None), P(("dp", "ctx"))
    return jax.shard_map(
        body,
        mesh=mesh,
        in_specs=(rows, rows, rows, rows, rows, flat, flat, P("dp"), P("dp")),
        out_specs=(rows, rows, rows, rows),
        check_vma=False,
    )
```

time: 492 us -> 106 us (0.22); the launches traced: 486 us -> 105 us
  waiting for transfers between devices: 186 us -> 0 us
  Pallas kernels: 0 us -> 98.2 us
  local copies, waits for them, and re-layouts: 88 us -> 6.24 us
  matrix products: 73.1 us -> 0 us
  other arithmetic: 54.6 us -> 0 us
  starting transfers between devices: 40.3 us -> 0 us
  between operations: 19.3 us -> 0.65 us
  loops' own time: 16.7 us -> 0 us
  blocking collectives: 8.32 us -> 0 us
    psum x2 -> x0, waiting for transfers between devices: 163 us -> none  [the longest x1 85 us: from_root(): return lax.psum(jnp.where(mine, array, jnp.zeros_like(array)), axis)]
    pallas_call x0 -> x1, Pallas kernels: none -> 98.2 us  [body(): pl.pallas_call(functools.partial(kernel, lax.axis_size('dp'), lax.axis_si...]
    dot_general x16 -> x0, matrix products: 73.1 us -> none  [the longest x2 15.6 us: block_step(): jnp.einsum('ihgd,sjhd->hgisj', query_block, slot_keys, preferred_element_...]
    ppermute x16 -> x0, starting transfers between devices: 40.2 us -> none  [from_behind(): lax.ppermute(array, axis, [(i, (i + by) % size) for i in range(size)])]
    ppermute x16 -> x0, waiting for transfers between devices: 22.5 us -> none  [from_behind(): lax.ppermute(array, axis, [(i, (i + by) % size) for i in range(size)])]
    reduce_sum x8 -> x0, other arithmetic: 21.6 us -> none  [the longest x2 16.2 us: block_step(): denominator = jnp.sum(exponent, axis=(3, 4), keepdims=True)]
    convert_element_type x4 -> x0, other arithmetic: 18.1 us -> none  [the longest x2 17.5 us: block_step(): prob_low = probability.astype(jnp.bfloat16)]
    gather x8 -> x0, local copies, waits for them, and re-layouts: 18 us -> none  [the longest x4 9.06 us: visit(): pool_keys[members]]
  transfers between devices with their start and end apart: 18 -> 0, of which waited for: 5 -> 0; matrix products, arithmetic and copies ran while one was open for 7% -> 0% of each run, Pallas kernels for 0% -> 0%
where the time goes in v1:
time: 106 us; the launch traced here: 105 us
  Pallas kernels  98.2 us (93%)
  local copies, waits for them, and re-layouts  6.24 us (6%)
    pallas_call x1, Pallas kernels, body(): pl.pallas_call(functools.partial(kernel, lax.axis_size('dp'), lax.axis_si...  98.2 us
    unnamed x10, local copies, waits for them, and re-layouts  6.24 us

profile of v1, /device:TPU:33, one launch (start us, length us, event | category | flops | bytes accessed | tf_op | source)
XLA Modules:
  0.0 105.1 jit_solution(10178794648392630554)
XLA Ops:
  0.6 98.2 %shard_map.120 = (bf16[256,4096]{1,0:T(8,128)(2,1)}, bf16[256,4096]{1,0:T(8,128)(2,1)}, f32[256,512]{1,0:T(8,128)}, f32[256,512]{1,0:T(8,128)}) custom-call(bf16[256,4096]{1,0:T(8,128)(2,1)} %q.1, bf16[256,512]{1,0:T(8,128)(2,1)} %k.1, bf16[256,512]{1,0:T(8,128)(2,1)} %v.1, bf16[256,4096]{1,0:T(8,128)(2,1)} %u.1, s32[2,6]{1,0:T(2,128)} %anc.1, ...), custom_call_target="tpu_custom_call" | custom-call | tf_op jit(solution)/shard_map/pallas_call | solution.py:491
  98.8 0.0 copy-start
  98.9 3.3 %copy.17 = bf16[256,4096]{1,0:T(8,128)(2,1)} copy(bf16[256,4096]{1,0:T(8,128)(2,1)} %get-tuple-element.8) | data formatting | bytes 4194304
  102.1 0.0 copy-done
  102.1 0.0 copy-start.2
  102.1 0.0 copy-start.1
  102.1 1.3 %copy.18 = bf16[256,4096]{1,0:T(8,128)(2,1)} copy(bf16[256,4096]{1,0:T(8,128)(2,1)S(1)} %copy-done) | data formatting | bytes 4194304
  103.5 0.1 copy-done.2
  103.5 0.8 copy.19
  104.3 0.0 copy-done.1
  104.3 0.8 copy.20
Async XLA Ops:
  98.8 3.3 %copy-start = (bf16[256,4096]{1,0:T(8,128)(2,1)S(1)}, bf16[256,4096]{1,0:T(8,128)(2,1)}, u32[]{:S(2)}) copy-start(bf16[256,4096]{1,0:T(8,128)(2,1)} %get-tuple-element.9) | copy-start | bytes 6291460
  102.1 1.4 %copy-start.2 = (f32[256,512]{1,0:T(8,128)S(1)}, f32[256,512]{1,0:T(8,128)}, u32[]{:S(2)}) copy-start(f32[256,512]{1,0:T(8,128)} %get-tuple-element.10) | copy-start | bytes 1572868
  102.1 2.2 %copy-start.1 = (f32[256,512]{1,0:T(8,128)S(1)}, f32[256,512]{1,0:T(8,128)}, u32[]{:S(2)}) copy-start(f32[256,512]{1,0:T(8,128)} %get-tuple-element.11) | copy-start | bytes 1572868

commit v2 on v1

--- a/solution.py
+++ b/solution.py
@@ -47,11 +47,20 @@
     mb=pltpu.VMEM((2, 2, W, W), F32),
     ku=pltpu.VMEM((4, N, W), BF16),
     vu=pltpu.VMEM((4, N, W), BF16),
-    pf=pltpu.VMEM((4, 4, N, 2 * W), F32),
-    dl=pltpu.VMEM((4, 4, 8, 2 * W), F32),
-    do=pltpu.VMEM((4, 4, 2 * W, W), BF16),
-    ps=pltpu.VMEM((N, 2 * W), F32),
-    acc=pltpu.VMEM((N, W), F32),
+    kt=pltpu.VMEM((4, W, N), BF16),
+    vt=pltpu.VMEM((4, W, N), BF16),
+    pf=pltpu.VMEM((16, N, 2 * W), F32),
+    dl=pltpu.VMEM((16, 8, 2 * W), F32),
+    do=pltpu.VMEM((16, 2 * W, W), BF16),
+    ps0=pltpu.VMEM((N, 2 * W), F32),
+    ps1=pltpu.VMEM((N, 2 * W), F32),
+    pk0=pltpu.VMEM((8, 2 * W), F32),
+    pk1=pltpu.VMEM((8, 2 * W), F32),
+    low0=pltpu.VMEM((N, 2 * W), BF16),
+    low1=pltpu.VMEM((N, 2 * W), BF16),
+    do0=pltpu.VMEM((2 * W, W), BF16),
+    do1=pltpu.VMEM((2 * W, W), BF16),
+    acc=pltpu.VMEM((4, N, W), F32),
     gacc=pltpu.VMEM((6, T, W), F32),
     pacc=pltpu.VMEM((T, W), F32),
     own=pltpu.VMEM((2, 2, T, W), F32),
@@ -297,90 +306,150 @@
             to[t, (2 + i) * W : (3 + i) * W] = picked.astype(BF16)
         to[t, 6 * W :] = s.kvp[kv, h, o + 4, pl.ds(pl.multiple_of(b * W, W), W), :]
 
-    def spread_block(t, h):
+    def spread_blocks(h):
+        def step(t, carry):
+            o, b = where_is(t, h)
+            s.pacc[...] += s.acc[t, 0 : 2 * W]
+            for i in range(HOPS):
+                chosen = jnp.broadcast_to(s.meta[o, b, 5 - i : 6 - i, :], (W, W)) == 1
+                x = s.acc[t, (2 + i) * W : (3 + i) * W]
+                s.gacc[o + i, 0:W] += jnp.where(chosen, 0.0, x)
+                s.gacc[o + i, W:] += jnp.where(chosen, x, 0.0)
+            s.gacc[o + 4, pl.ds(pl.multiple_of(b * W, W), W), :] += s.acc[t, 6 * W :]
+            return carry
+
+        lax.fori_loop(0, 4, step, 0)
+
+    def chunk(j, h):
+        t = j // 4
         o, b = where_is(t, h)
-        s.pacc[...] += s.acc[0 : 2 * W]
-        for i in range(HOPS):
-            chosen = jnp.broadcast_to(s.meta[o, b, 5 - i : 6 - i, :], (W, W)) == 1
-            x = s.acc[(2 + i) * W : (3 + i) * W]
-            s.gacc[o + i, 0:W] += jnp.where(chosen, 0.0, x)
-            s.gacc[o + i, W:] += jnp.where(chosen, x, 0.0)
-        s.gacc[o + 4, pl.ds(pl.multiple_of(b * W, W), W), :] += s.acc[6 * W :]
+        return t, o, b, lax.rem(j, 4)
 
     def pair(ref, o, h, b, g):
         rows = pl.ds(pl.multiple_of(b * W, W), W)
-        return [ref.at[o, h, rows, pl.ds((2 * g + i) * W, W)] for i in range(2)]
+        return [
+            ref.at[o, h, rows, pl.ds(pl.multiple_of((2 * g + i) * W, W), W)] for i in range(2)
+        ]
+
+    def joined(ref, o, h, b, g):
+        return jnp.concatenate([x[...] for x in pair(ref, o, h, b, g)], axis=0)
+
+    def twice(row):
+        return jnp.concatenate([row, row], axis=1)
+
+    META_ROWS = (0, 1, 5, 4, 3, 2)
+
+    def biases(o, b):
+        rows = []
+        for i in range(6):
+            row = s.meta[o, b, META_ROWS[i] : META_ROWS[i] + 1, :]
+            unseen = row <= 0 if i < 2 else row < 0
+            rows.append(twice(jnp.where(unseen, -jnp.inf, 0.0)))
+        return rows
+
+    def score(j, h, ps, pk):
+        t, o, b, g = chunk(j, h)
+        scores = nt(s.ku[t], joined(s.qb, o, h, b, g))
+        seen = scores[6 * W :] + twice(s.mb[o, b])
+        peak = jnp.max(seen, axis=0, keepdims=True)
+        for i, bias in enumerate(biases(o, b)):
+            top = jnp.max(scores[i * W : (i + 1) * W], axis=0, keepdims=True)
+            peak = jnp.maximum(peak, top + bias)
+        ps[0 : 6 * W] = scores[0 : 6 * W]
+        ps[6 * W :] = seen
+        pk[0:1] = peak * exp_scale
+
+    def soften(j, h, ps, pk, low, do):
+        t, o, b, g = chunk(j, h)
+        shift = pk[0:1]
+        bias = biases(o, b)
+        denominator = jnp.zeros((1, 2 * W), F32)
+        for i in range(7):
+            here = shift if i == 6 else shift - bias[i]
+            e = jnp.exp2(ps[i * W : (i + 1) * W] * exp_scale - here)
+            ps[i * W : (i + 1) * W] = e
+            denominator = denominator + jnp.sum(e, axis=0, keepdims=True)
+        inverse = 1.0 / denominator
+        for i in range(7):
+            probs = ps[i * W : (i + 1) * W] * inverse
+            s.pf[j, i * W : (i + 1) * W] = probs
+            low[i * W : (i + 1) * W] = probs.astype(BF16)
+        weight = s.wt[o, b]
+        up = [x[...].astype(F32) * weight for x in pair(s.ub, o, h, b, g)]
+        grad_out = jnp.concatenate(up, axis=0).astype(BF16)
+        do[...] = grad_out
+        s.do[j] = grad_out
+
+    def attend(j, h, low, do):
+        t, o, b, g = chunk(j, h)
+        attended = jnp.transpose(nn(s.vt[t], low[...])).astype(BF16)
+        s.acc[t] += nn(low[...], do[...])
+        for i, x in enumerate(pair(s.ob, o, h, b, g)):
+            x[...] = attended[i * W : (i + 1) * W]
+        product = do[...].astype(F32) * attended.astype(F32)
+        s.dl[j, 0:1] = jnp.sum(jnp.transpose(product), axis=0, keepdims=True)
 
     def forward(h):
-        def step(t, carry):
-            o, b = where_is(t, h)
+        def prepare(t, carry):
             gather_block(t, h, K_, s.ku)
             gather_block(t, h, V_, s.vu)
-            bias = []
-            for i in range(6):
-                row = s.meta[o, b, (0, 1, 5, 4, 3, 2)[i] : (0, 1, 5, 4, 3, 2)[i] + 1, :]
-                unseen = row <= 0 if i < 2 else row < 0
-                row = jnp.where(unseen, -jnp.inf, 0.0)
-                bias.append(jnp.concatenate([row, row], axis=1))
-            mask = jnp.concatenate([s.mb[o, b], s.mb[o, b]], axis=1)
-            weight = s.wt[o, b]
-            for g in range(4):
-                queries = jnp.concatenate([x[...] for x in pair(s.qb, o, h, b, g)], axis=0)
-                scores = nt(s.ku[t], queries)
-                s.ps[0 : 6 * W] = scores[0 : 6 * W]
-                s.ps[6 * W :] = scores[6 * W :] + mask
-                peak = jnp.max(s.ps[6 * W :], axis=0, keepdims=True)
-                for i in range(6):
-                    top = jnp.max(s.ps[i * W : (i + 1) * W], axis=0, keepdims=True)
-                    peak = jnp.maximum(peak, top + bias[i])
-                shift = peak * exp_scale
-                denominator = jnp.zeros((1, 2 * W), F32)
-                for i in range(7):
-                    here = shift if i == 6 else shift - bias[i]
-                    e = jnp.exp2(s.ps[i * W : (i + 1) * W] * exp_scale - here)
-                    s.ps[i * W : (i + 1) * W] = e
-                    denominator = denominator + jnp.sum(e, axis=0, keepdims=True)
-                probs = s.ps[...] * (1.0 / denominator)
-                s.pf[t, g] = probs
-                low = probs.astype(BF16)
-                up = [x[...].astype(F32) * weight for x in pair(s.ub, o, h, b, g)]
-                grad_out = jnp.concatenate(up, axis=0).astype(BF16)
-                s.do[t, g] = grad_out
-                attended = jnp.transpose(tn(s.vu[t], low)).astype(BF16)
-                for i, x in enumerate(pair(s.ob, o, h, b, g)):
-                    x[...] = attended[i * W : (i + 1) * W]
-                product = grad_out.astype(F32) * attended.astype(F32)
-                s.dl[t, g, 0:1] = jnp.sum(jnp.transpose(product), axis=0, keepdims=True)
-                term = nn(low, grad_out)
-                if g == 0:
-                    s.acc[...] = term
-                else:
-                    s.acc[...] += term
-            spread_block(t, h)
+            s.kt[t] = jnp.transpose(s.ku[t])
+            s.vt[t] = jnp.transpose(s.vu[t])
             return carry
 
-        lax.fori_loop(0, 4, step, 0)
+        lax.fori_loop(0, 4, prepare, 0)
+        s.acc[...] = jnp.zeros_like(s.acc)
+        even, odd = (s.ps0, s.pk0), (s.ps1, s.pk1)
+        low_even, low_odd = (s.low0, s.do0), (s.low1, s.do1)
+        score(0, h, *even)
+        score(1, h, *odd)
+        soften(0, h, *even, *low_even)
+
+        def step(i, carry):
+            j = 2 * i
+            attend(j - 2, h, *low_even)
+            score(j, h, *even)
+            soften(j - 1, h, *odd, *low_odd)
+            attend(j - 1, h, *low_odd)
+            score(j + 1, h, *odd)
+            soften(j, h, *even, *low_even)
+            return carry
+
+        lax.fori_loop(1, 8, step, 0)
+        attend(14, h, *low_even)
+        soften(15, h, *odd, *low_odd)
+        attend(15, h, *low_odd)
+        spread_blocks(h)
+
+    def score_grad(j, h, low):
+        t, o, b, g = chunk(j, h)
+        dprobs = nt(s.vu[t], s.do[j])
+        low[...] = (s.pf[j] * (dprobs - s.dl[j, 0:1]) * inv_root).astype(BF16)
+
+    def input_grads(j, h, low):
+        t, o, b, g = chunk(j, h)
+        grad = jnp.transpose(nn(s.kt[t], low[...])).astype(BF16)
+        s.acc[t] += nn(low[...], joined(s.qb, o, h, b, g))
+        for i, x in enumerate(pair(s.gb, o, h, b, g)):
+            x[...] = grad[i * W : (i + 1) * W]
 
     def backward(h):
-        def step(t, carry):
-            o, b = where_is(t, h)
-            for g in range(4):
-                queries = jnp.concatenate([x[...] for x in pair(s.qb, o, h, b, g)], axis=0)
-                dprobs = nt(s.vu[t], s.do[t, g])
-                dscores = s.pf[t, g] * (dprobs - s.dl[t, g, 0:1]) * inv_root
-                dscores = dscores.astype(BF16)
-                grad = jnp.transpose(tn(s.ku[t], dscores)).astype(BF16)
-                for i, x in enumerate(pair(s.gb, o, h, b, g)):
-                    x[...] = grad[i * W : (i + 1) * W]
-                term = nn(dscores, queries)
-                if g == 0:
-                    s.acc[...] = term
-                else:
-                    s.acc[...] += term
-            spread_block(t, h)
+        s.acc[...] = jnp.zeros_like(s.acc)
+        score_grad(0, h, s.low0)
+
+        def step(i, carry):
+            j = 2 * i
+            score_grad(j + 1, h, s.low1)
+            input_grads(j, h, s.low0)
+            score_grad(j + 2, h, s.low0)
+            input_grads(j + 1, h, s.low1)
             return carry
 
-        lax.fori_loop(0, 4, step, 0)
+        lax.fori_loop(0, 7, step, 0)
+        score_grad(15, h, s.low1)
+        input_grads(14, h, s.low0)
+        input_grads(15, h, s.low1)
+        spread_blocks(h)
 
     def clear():
         s.gacc[...] = jnp.zeros_like(s.gacc)
@@ -484,23 +553,32 @@
             await_bytes(s.prec.at[i, h, pl.ds(0, chips - 1)], s.ps_send.at[i, h])
 
 
+def write_out(*refs):
+    sems = refs[8]
+    copies = [pltpu.make_async_copy(refs[i], refs[4 + i], sems.at[i]) for i in range(4)]
+    for copy in copies:
+        copy.start()
+    for copy in copies:
+        copy.wait()
+
+
 def body(queries, keys, values, upstream, ancestors, segments, responses, rewards, lengths):
-    any_spec = pl.BlockSpec(memory_space=pl.ANY)
+    any_spec = pl.BlockSpec(memory_space=pltpu.HBM)
     smem = pl.BlockSpec(memory_space=pltpu.SMEM)
     vmem = pl.BlockSpec(memory_space=pltpu.VMEM)
-    return pl.pallas_call(
+    results = pl.pallas_call(
         functools.partial(kernel, lax.axis_size("dp"), lax.axis_size("ctx")),
         out_shape=[
-            jax.ShapeDtypeStruct(queries.shape, BF16),
-            jax.ShapeDtypeStruct(queries.shape, BF16),
-            jax.ShapeDtypeStruct(keys.shape, F32),
-            jax.ShapeDtypeStruct(keys.shape, F32),
+            pltpu.VMEM(queries.shape, BF16),
+            pltpu.VMEM(queries.shape, BF16),
+            pltpu.VMEM(keys.shape, F32),
+            pltpu.VMEM(keys.shape, F32),
         ],
         in_specs=[any_spec] * 4 + [smem, vmem, vmem, smem, smem],
         out_specs=[vmem] * 4,
         scratch_shapes=list(SCRATCH.values()),
         compiler_params=pltpu.CompilerParams(
-            collective_id=0, has_side_effects=True, vmem_limit_bytes=60 * 1024 * 1024
+            collective_id=0, has_side_effects=True, vmem_limit_bytes=56 * 1024 * 1024
         ),
     )(
         queries,
@@ -513,6 +591,13 @@
         rewards,
         lengths,
     )
+    return pl.pallas_call(
+        write_out,
+        out_shape=[jax.ShapeDtypeStruct(x.shape, x.dtype) for x in results],
+        in_specs=[vmem] * 4,
+        out_specs=[any_spec] * 4,
+        scratch_shapes=[pltpu.SemaphoreType.DMA((4,))],
+    )(*results)
 
 
 def solution(mesh):

time: 106 us -> 103 us (0.972)
  local copies, waits for them, and re-layouts: 6.24 us -> 4.25 us
    pallas_call x1, Pallas kernels: 98.2 us -> 92.4 us  [body(): pl.pallas_call(functools.partial(kernel, lax.axis_size('dp'), lax.axis_si...]
    pallas_call x0 -> x1, Pallas kernels: none -> 4.82 us  [body(): pl.pallas_call(write_out, out_shape=[jax.ShapeDtypeStruct(x.shape, x.dtyp...]
    unnamed x10 -> x8, local copies, waits for them, and re-layouts: 6.24 us -> 4.25 us
where the time goes in v2:
time: 103 us; the launch traced here: 102 us
  Pallas kernels  97.2 us (94%)
  local copies, waits for them, and re-layouts  4.25 us (4%)
    pallas_call x1, Pallas kernels, body(): pl.pallas_call(functools.partial(kernel, lax.axis_size('dp'), lax.axis_si...  92.4 us
    pallas_call x1, Pallas kernels, body(): pl.pallas_call(write_out, out_shape=[jax.ShapeDtypeStruct(x.shape, x.dtyp...  4.82 us
    unnamed x8, local copies, waits for them, and re-layouts  4.25 us

profile of v2, /device:TPU:33, one launch (start us, length us, event | category | flops | bytes accessed | tf_op | source)
XLA Modules:
  0.0 102.1 jit_solution(3359218663142304678)
XLA Ops:
  0.6 92.4 %shard_map.120 = (bf16[256,4096]{1,0:T(8,128)(2,1)S(1)}, bf16[256,4096]{1,0:T(8,128)(2,1)S(1)}, f32[256,512]{1,0:T(8,128)S(1)}, f32[256,512]{1,0:T(8,128)S(1)}) custom-call(bf16[256,4096]{1,0:T(8,128)(2,1)} %q.1, bf16[256,512]{1,0:T(8,128)(2,1)} %k.1, bf16[256,512]{1,0:T(8,128)(2,1)} %v.1, bf16[256,4096]{1,0:T(8,128)(2,1)} %u.1, s32[2,6]{1,0:T(2,128)} %anc.1, ...), custom_call_target="tpu_custom_call" | custom-call | tf_op jit(solution)/shard_map/pallas_call | solution.py:569
  93.0 0.0 copy-start
  93.0 1.3 %copy-done = bf16[256,4096]{1,0:T(8,128)(2,1)} copy-done((bf16[256,4096]{1,0:T(8,128)(2,1)}, bf16[256,4096]{1,0:T(8,128)(2,1)S(1)}, u32[]{:S(2)}) %copy-start) | copy-done | bytes 2097176
  94.4 0.0 copy-start.1
  94.4 1.3 %copy-done.1 = bf16[256,4096]{1,0:T(8,128)(2,1)} copy-done((bf16[256,4096]{1,0:T(8,128)(2,1)}, bf16[256,4096]{1,0:T(8,128)(2,1)S(1)}, u32[]{:S(2)}) %copy-start.1) | copy-done | bytes 2097176
  95.7 0.0 copy-start.2
  95.7 0.8 copy-done.2
  96.5 0.0 copy-start.3
  96.5 0.8 copy-done.3
  97.3 4.8 %shard_map.121 = (bf16[256,4096]{1,0:T(8,128)(2,1)}, bf16[256,4096]{1,0:T(8,128)(2,1)}, f32[256,512]{1,0:T(8,128)}, f32[256,512]{1,0:T(8,128)}) custom-call(bf16[256,4096]{1,0:T(8,128)(2,1)} %copy-done, bf16[256,4096]{1,0:T(8,128)(2,1)} %copy-done.1, f32[256,512]{1,0:T(8,128)} %copy-done.2, f32[256,512]{1,0:T(8,128)} %copy-done.3), custom_call_target="tpu_custom_call" | custom-call | tf_op jit(solution)/shard_map/pallas_call | solution.py:594
Async XLA Ops:
  93.0 1.3 %copy-start = (bf16[256,4096]{1,0:T(8,128)(2,1)}, bf16[256,4096]{1,0:T(8,128)(2,1)S(1)}, u32[]{:S(2)}) copy-start(bf16[256,4096]{1,0:T(8,128)(2,1)S(1)} %get-tuple-element.8.refs_0_) | copy-start | bytes 6291460
  94.4 1.3 %copy-start.1 = (bf16[256,4096]{1,0:T(8,128)(2,1)}, bf16[256,4096]{1,0:T(8,128)(2,1)S(1)}, u32[]{:S(2)}) copy-start(bf16[256,4096]{1,0:T(8,128)(2,1)S(1)} %get-tuple-element.9.refs_1_) | copy-start | bytes 6291460
  95.7 0.8 copy-start.2
  96.5 0.8 copy-start.3

commit v3 on v2

--- a/solution.py
+++ b/solution.py
@@ -37,10 +37,11 @@
     ub=pltpu.VMEM((2, 2, T, C), BF16),
     ob=pltpu.VMEM((2, 2, T, C), BF16),
     gb=pltpu.VMEM((2, 2, T, C), BF16),
-    cand=pltpu.VMEM((16, 2, 2, 16, W), BF16),
-    scat=pltpu.VMEM((16, 2, 2, 16, W), BF16),
+    cand=pltpu.VMEM((2, 16, 2, 16, W), BF16),
+    scat0=pltpu.VMEM((16, 2, 16, W), BF16),
+    scat1=pltpu.VMEM((16, 2, 16, W), BF16),
     sel=pltpu.VMEM((2, 2, 16, W), BF16),
-    gath=pltpu.VMEM((16, 2, 2, 16, W), BF16),
+    gath=pltpu.VMEM((2, 16, 2, 16, W), BF16),
     meta=pltpu.VMEM((2, 2, 8, W), jnp.int32),
     lens=pltpu.VMEM((4, 8, W), jnp.int32),
     wt=pltpu.VMEM((2, 2, W, W), F32),
@@ -71,7 +72,7 @@
     psend=pltpu.VMEM((2, 2, 16, 16, W), BF16),
     prec=pltpu.VMEM((2, 2, 16, 16, W), BF16),
     agsend=pltpu.VMEM((2, 2, 16, W), BF16),
-    ag=pltpu.VMEM((2, 32, 2, 16, W), BF16),
+    ag=pltpu.VMEM((2, 2, 32, 16, W), BF16),
     one_send=pltpu.SemaphoreType.DMA((64,)),
     local=pltpu.SemaphoreType.DMA((12,)),
     kv_recv=pltpu.SemaphoreType.DMA((2, 2)),
@@ -81,14 +82,14 @@
     lens_recv=pltpu.SemaphoreType.DMA,
     qu_recv=pltpu.SemaphoreType.DMA((2, 2)),
     out_recv=pltpu.SemaphoreType.DMA((2, 2)),
-    pr_send=pltpu.SemaphoreType.DMA((2,)),
-    pr_recv=pltpu.SemaphoreType.DMA((2,)),
+    pr_send=pltpu.SemaphoreType.DMA((2, 2)),
+    pr_recv=pltpu.SemaphoreType.DMA((2, 2)),
     g_recv=pltpu.SemaphoreType.DMA((2, 2)),
     m_recv=pltpu.SemaphoreType.DMA((2, 2)),
     ps_send=pltpu.SemaphoreType.DMA((2, 2)),
     ps_recv=pltpu.SemaphoreType.DMA((2, 2)),
-    ag_send=pltpu.SemaphoreType.DMA((2,)),
-    ag_recv=pltpu.SemaphoreType.DMA((2,)),
+    ag_send=pltpu.SemaphoreType.DMA((2, 2)),
+    ag_recv=pltpu.SemaphoreType.DMA((2, 2)),
 )
 
 
@@ -113,6 +114,7 @@
     root_chip, root_core = lax.div(root, 2), lax.rem(root, 2)
 
     sends = []
+    scat = (s.scat0, s.scat1)
 
     def send(src, dst, recv_sem, to):
         copy = pltpu.make_async_remote_copy(
@@ -204,32 +206,22 @@
         ).start()
     send(s.meta.at[core], s.meta.at[core], s.meta_recv, mate)
 
-    def send_chain(h):
-        for kv, src in ((K_, k), (V_, v)):
-            for hop in (1, 2):
-                for lane in range(2):
-                    send(
-                        src.at[:, kcols(lane, h)],
-                        s.kvp.at[kv, h, 2 * (2 - hop) + core],
-                        s.kv_recv.at[kv, h],
-                        2 * lax.rem(chip + hop, chips) + lane,
-                    )
+    def send_chain(h, kv, hop):
+        for lane in range(2):
+            send(
+                (k, v)[kv].at[:, kcols(lane, h)],
+                s.kvp.at[kv, h, 2 * (2 - hop) + core],
+                s.kv_recv.at[kv, h],
+                2 * lax.rem(chip + hop, chips) + lane,
+            )
 
     def send_qu(h):
         send(q.at[:, qcols(other, h)], s.qb.at[core, h], s.qu_recv.at[h, 0], mate)
         send(u.at[:, qcols(other, h)], s.ub.at[core, h], s.qu_recv.at[h, 1], mate)
 
-    send_chain(0)
-    send_qu(0)
-
     for copy in own_kv:
         copy.wait()
     await_bytes(s.kvp.at[0, 0, pl.ds(0, 4)], s.mate_kv)
-    for h in range(2):
-        for kv in range(2):
-            x = lax.select(root_core == 0, s.kvp[kv, h, 4], s.kvp[kv, h, 5])
-            s.cand[:, h, kv] = x.reshape(16, 16, W)
-
     def to_chips(start):
         def step(i, carry):
             start(lax.rem(chip + i, chips))
@@ -247,14 +239,22 @@
             device_id_type=MESH,
         ).start()
 
-    to_chips(
-        lambda c: loop_send(
-            s.cand.at[c], s.scat.at[chip], s.pr_send.at[0], s.pr_recv.at[0], 2 * c + core
+    for h in range(2):
+        for kv in range(2):
+            x = lax.select(root_core == 0, s.kvp[kv, h, 4], s.kvp[kv, h, 5])
+            s.cand[h, :, kv] = x.reshape(16, 16, W)
+        scat[h][chip] = s.cand[h, chip]
+        to_chips(
+            lambda c, h=h: loop_send(
+                s.cand.at[h, c],
+                scat[h].at[chip],
+                s.pr_send.at[0, h],
+                s.pr_recv.at[0, h],
+                2 * c + core,
+            )
         )
-    )
-    s.scat[chip] = s.cand[chip]
-    send_chain(1)
-    send_qu(1)
+    send_chain(0, K_, 1)
+    send_qu(0)
 
     await_bytes(s.meta.at[0], s.meta_recv)
     await_bytes(s.lens.at[pl.ds(0, groups - 1)], s.lens_recv)
@@ -285,20 +285,35 @@
             seen = seen | (key_row == query_col)
             s.mb[o, b] = jnp.where(seen, 0.0, -jnp.inf)
 
-    await_bytes(s.scat.at[pl.ds(0, chips - 1)], s.pr_recv.at[0])
-    prompt_slice = s.scat[root_chip]
-    s.sel[...] = prompt_slice
-    s.gath[chip] = prompt_slice
-    to_chips(
-        lambda c: loop_send(s.sel, s.gath.at[chip], s.pr_send.at[1], s.pr_recv.at[1], 2 * c + core)
-    )
+    for h in range(2):
+        await_bytes(scat[h].at[pl.ds(0, chips - 1)], s.pr_recv.at[0, h])
+        prompt_slice = scat[h][root_chip]
+        s.sel[h] = prompt_slice
+        s.gath[h, chip] = prompt_slice
+        to_chips(
+            lambda c, h=h: loop_send(
+                s.sel.at[h],
+                s.gath.at[h, chip],
+                s.pr_send.at[1, h],
+                s.pr_recv.at[1, h],
+                2 * c + core,
+            )
+        )
+        if h == 0:
+            send_chain(0, K_, 2)
+            send_chain(0, V_, 1)
+            send_chain(0, V_, 2)
+    for kv in range(2):
+        send_chain(1, kv, 1)
+        send_chain(1, kv, 2)
+    send_qu(1)
 
     def where_is(t, h):
         return lax.rem(core + t // 2 + h, 2), lax.rem(t, 2)
 
     def gather_block(t, h, kv, to):
         o, b = where_is(t, h)
-        to[t, 0 : 2 * W] = s.gath[:, h, kv].reshape(T, W)
+        to[t, 0 : 2 * W] = s.gath[h, :, kv].reshape(T, W)
         for i in range(HOPS):
             chosen = s.meta[o, b, 5 - i : 6 - i, :]
             both = s.kvp[kv, h, o + i].astype(F32)
@@ -456,15 +471,6 @@
         s.pacc[...] = jnp.zeros_like(s.pacc)
 
     def send_grads(kv, h):
-        for i in range(4):
-            s.gsend[kv, h, i] = s.gacc[i].astype(BF16)
-            hop = 2 if i < 2 else 1
-            send(
-                s.gsend.at[kv, h, i],
-                s.grecv.at[kv, h, hop - 1, core],
-                s.g_recv.at[kv, h],
-                2 * lax.rem(chip - hop + chips, chips) + i % 2,
-            )
         s.psend[kv, h] = s.pacc[...].reshape(16, 16, W).astype(BF16)
         to_chips(
             lambda c: loop_send(
@@ -476,6 +482,15 @@
             )
         )
         s.prec[kv, h, chip] = s.psend[kv, h, chip]
+        for i in range(4):
+            s.gsend[kv, h, i] = s.gacc[i].astype(BF16)
+            hop = 2 if i < 2 else 1
+            send(
+                s.gsend.at[kv, h, i],
+                s.grecv.at[kv, h, hop - 1, core],
+                s.g_recv.at[kv, h],
+                2 * lax.rem(chip - hop + chips, chips) + i % 2,
+            )
         s.msend[kv, h] = s.gacc[4 + other]
         send(s.msend.at[kv, h], s.mrecv.at[kv, h], s.m_recv.at[kv, h], mate)
         s.own[kv, h] = s.gacc[4 + core]
@@ -486,40 +501,38 @@
         send(staged.at[other, h], out.at[:, qcols(core, h)], recv_sem, mate)
         own_out.append(fetch(staged.at[core, h], out.at[:, qcols(core, h)]))
 
-    def sum_prompt(h):
-        for kv in range(2):
-            await_bytes(s.prec.at[kv, h, pl.ds(0, chips - 1)], s.ps_recv.at[kv, h])
-            summed = jnp.sum(s.prec[kv, h].astype(F32), axis=0).astype(BF16)
-            s.agsend[h, kv] = summed
-            s.ag[h, 16 * core + chip, kv] = summed
+    def sum_prompt(kv, h):
+        await_bytes(s.prec.at[kv, h, pl.ds(0, chips - 1)], s.ps_recv.at[kv, h])
+        summed = jnp.sum(s.prec[kv, h].astype(F32), axis=0).astype(BF16)
+        s.agsend[kv, h] = summed
+        s.ag[kv, h, 16 * core + chip] = summed
 
         def step(i, carry):
             loop_send(
-                s.agsend.at[h],
-                s.ag.at[h, 16 * core + chip],
-                s.ag_send.at[h],
-                s.ag_recv.at[h],
+                s.agsend.at[kv, h],
+                s.ag.at[kv, h, 16 * core + chip],
+                s.ag_send.at[kv, h],
+                s.ag_recv.at[kv, h],
                 lax.rem(me + i, ring),
             )
             return carry
 
         lax.fori_loop(1, ring, step, 0)
 
-    def finish(h):
-        await_bytes(s.ag.at[h, pl.ds(0, ring - 1)], s.ag_recv.at[h])
-        for kv, out in ((K_, gk), (V_, gv)):
-            await_bytes(s.grecv.at[kv, h], s.g_recv.at[kv, h])
-            await_bytes(s.mrecv.at[kv, h], s.m_recv.at[kv, h])
-            for lane, mine in ((core, s.own), (other, s.mrecv)):
-                x = mine[kv, h] + s.grecv[kv, h, 0, lane].astype(F32)
-                x = x + s.grecv[kv, h, 1, lane].astype(F32)
-                prompt = s.ag[h, pl.ds(16 * lane, 16), kv].astype(F32).reshape(T, W)
-                here = jnp.full((T, W), root, jnp.int32) == me
-                out[:, kcols(lane, h)] = x + jnp.where(here, prompt, 0.0)
+    def finish(kv, h):
+        out = (gk, gv)[kv]
+        await_bytes(s.grecv.at[kv, h], s.g_recv.at[kv, h])
+        await_bytes(s.mrecv.at[kv, h], s.m_recv.at[kv, h])
+        await_bytes(s.ag.at[kv, h, pl.ds(0, ring - 1)], s.ag_recv.at[kv, h])
+        for lane, mine in ((core, s.own), (other, s.mrecv)):
+            x = mine[kv, h] + s.grecv[kv, h, 0, lane].astype(F32)
+            x = x + s.grecv[kv, h, 1, lane].astype(F32)
+            prompt = s.ag[kv, h, pl.ds(16 * lane, 16)].astype(F32).reshape(T, W)
+            here = jnp.full((T, W), root, jnp.int32) == me
+            out[:, kcols(lane, h)] = x + jnp.where(here, prompt, 0.0)
 
     for h in range(2):
-        if h == 0:
-            await_bytes(s.gath.at[pl.ds(0, chips - 1)], s.pr_recv.at[1])
+        await_bytes(s.gath.at[h, pl.ds(0, chips - 1)], s.pr_recv.at[1, h])
         for kv in range(2):
             await_bytes(s.kvp.at[kv, h, pl.ds(0, 4)], s.kv_recv.at[kv, h])
             await_bytes((s.qb, s.ub)[kv].at[other, h], s.qu_recv.at[h, kv])
@@ -529,14 +542,17 @@
         send_grads(V_, h)
         send_rows(s.ob, attn, h, s.out_recv.at[0, h])
         if h == 1:
-            sum_prompt(0)
+            sum_prompt(K_, 0)
         clear()
         backward(h)
         send_grads(K_, h)
+        sum_prompt(V_, h)
         send_rows(s.gb, gq, h, s.out_recv.at[1, h])
-    finish(0)
-    sum_prompt(1)
-    finish(1)
+    finish(V_, 0)
+    finish(K_, 0)
+    finish(V_, 1)
+    sum_prompt(K_, 1)
+    finish(K_, 1)
 
     for copy in own_out:
         copy.wait()
@@ -547,9 +563,9 @@
         copy.wait_send()
     await_bytes(s.lens.at[pl.ds(0, groups - 1)], s.lens_send)
     for i in range(2):
-        await_bytes(s.scat.at[pl.ds(0, chips - 1)], s.pr_send.at[i])
-        await_bytes(s.ag.at[i, pl.ds(0, ring - 1)], s.ag_send.at[i])
         for h in range(2):
+            await_bytes(s.gath.at[h, pl.ds(0, chips - 1)], s.pr_send.at[i, h])
+            await_bytes(s.ag.at[i, h, pl.ds(0, ring - 1)], s.ag_send.at[i, h])
             await_bytes(s.prec.at[i, h, pl.ds(0, chips - 1)], s.ps_send.at[i, h])
 
 
@@ -597,7 +613,8 @@
         in_specs=[vmem] * 4,
         out_specs=[any_spec] * 4,
         scratch_shapes=[pltpu.SemaphoreType.DMA((4,))],
-    )(*results)
+        compiler_params=pltpu.CompilerParams(vmem_limit_bytes=1024 * 1024),
+    )(*[pltpu.with_memory_space_constraint(x, pltpu.VMEM) for x in results])
 
 
 def solution(mesh):

time: 103 us -> 86.1 us (0.84)
  the two profiles are of different devices: /device:TPU:33 before, /device:TPU:1 now
where the time goes in v3:
time: 86.1 us; the launch traced here: 86 us
  Pallas kernels  85.3 us (99%)
    pallas_call x1, Pallas kernels, body(): pl.pallas_call(functools.partial(kernel, lax.axis_size('dp'), lax.axis_si...  82.9 us
    pallas_call x1, Pallas kernels, body(): pl.pallas_call(write_out, out_shape=[jax.ShapeDtypeStruct(x.shape, x.dtyp...  2.37 us

profile of v3, /device:TPU:1, one launch (start us, length us, event | category | flops | bytes accessed | tf_op | source)
XLA Modules:
  0.0 86.0 jit_solution(17719161281097354271)
XLA Ops:
  0.6 82.9 %shard_map.120 = (bf16[256,4096]{1,0:T(8,128)(2,1)S(1)}, bf16[256,4096]{1,0:T(8,128)(2,1)S(1)}, f32[256,512]{1,0:T(8,128)S(1)}, f32[256,512]{1,0:T(8,128)S(1)}) custom-call(bf16[256,4096]{1,0:T(8,128)(2,1)} %q.1, bf16[256,512]{1,0:T(8,128)(2,1)} %k.1, bf16[256,512]{1,0:T(8,128)(2,1)} %v.1, bf16[256,4096]{1,0:T(8,128)(2,1)} %u.1, s32[2,6]{1,0:T(2,128)} %anc.1, ...), custom_call_target="tpu_custom_call" | custom-call | tf_op jit(solution)/shard_map/pallas_call | solution.py:585
  83.6 2.4 %shard_map.121 = (bf16[256,4096]{1,0:T(8,128)(2,1)}, bf16[256,4096]{1,0:T(8,128)(2,1)}, f32[256,512]{1,0:T(8,128)}, f32[256,512]{1,0:T(8,128)}) custom-call(bf16[256,4096]{1,0:T(8,128)(2,1)S(1)} %get-tuple-element.8.refs_0_, bf16[256,4096]{1,0:T(8,128)(2,1)S(1)} %get-tuple-element.9.refs_1_, f32[256,512]{1,0:T(8,128)S(1)} %get-tuple-element.10.refs_2_, ...), custom_call_target="tpu_custom_call" | custom-call | tf_op jit(solution)/shard_map/pallas_call | solution.py:610

commit v4 on v3

--- a/solution.py
+++ b/solution.py
@@ -17,6 +17,7 @@
 N = 7 * W
 HOPS = 4
 K_, V_ = 0, 1
+CUTS = ((0, 4), (4, 7))
 
 
 def nn(a, b):
@@ -76,6 +77,7 @@
     one_send=pltpu.SemaphoreType.DMA((64,)),
     local=pltpu.SemaphoreType.DMA((12,)),
     kv_recv=pltpu.SemaphoreType.DMA((2, 2)),
+    kv_relay=pltpu.SemaphoreType.DMA((2, 2)),
     mate_kv=pltpu.SemaphoreType.DMA,
     meta_recv=pltpu.SemaphoreType.DMA,
     lens_send=pltpu.SemaphoreType.DMA,
@@ -206,18 +208,29 @@
         ).start()
     send(s.meta.at[core], s.meta.at[core], s.meta_recv, mate)
 
-    def send_chain(h, kv, hop):
+    def send_chain(h, kv):
         for lane in range(2):
             send(
                 (k, v)[kv].at[:, kcols(lane, h)],
-                s.kvp.at[kv, h, 2 * (2 - hop) + core],
+                s.kvp.at[kv, h, 2 + core],
                 s.kv_recv.at[kv, h],
-                2 * lax.rem(chip + hop, chips) + lane,
+                2 * lax.rem(chip + 1, chips) + lane,
             )
+
+    def relay_chain(h, kv):
+        await_bytes(s.kvp.at[kv, h, pl.ds(2, 2)], s.kv_recv.at[kv, h])
+        send(
+            s.kvp.at[kv, h, pl.ds(2, 2)],
+            s.kvp.at[kv, h, pl.ds(0, 2)],
+            s.kv_relay.at[kv, h],
+            2 * lax.rem(chip + 1, chips) + core,
+        )
 
     def send_qu(h):
         send(q.at[:, qcols(other, h)], s.qb.at[core, h], s.qu_recv.at[h, 0], mate)
         send(u.at[:, qcols(other, h)], s.ub.at[core, h], s.qu_recv.at[h, 1], mate)
+
+    send_chain(0, K_)
 
     for copy in own_kv:
         copy.wait()
@@ -253,7 +266,8 @@
                 2 * c + core,
             )
         )
-    send_chain(0, K_, 1)
+        if h == 0:
+            send_chain(0, V_)
     send_qu(0)
 
     await_bytes(s.meta.at[0], s.meta_recv)
@@ -300,12 +314,10 @@
             )
         )
         if h == 0:
-            send_chain(0, K_, 2)
-            send_chain(0, V_, 1)
-            send_chain(0, V_, 2)
+            relay_chain(0, K_)
+            relay_chain(0, V_)
     for kv in range(2):
-        send_chain(1, kv, 1)
-        send_chain(1, kv, 2)
+        send_chain(1, kv)
     send_qu(1)
 
     def where_is(t, h):
@@ -364,14 +376,20 @@
 
     def score(j, h, ps, pk):
         t, o, b, g = chunk(j, h)
-        scores = nt(s.ku[t], joined(s.qb, o, h, b, g))
-        seen = scores[6 * W :] + twice(s.mb[o, b])
-        peak = jnp.max(seen, axis=0, keepdims=True)
-        for i, bias in enumerate(biases(o, b)):
-            top = jnp.max(scores[i * W : (i + 1) * W], axis=0, keepdims=True)
-            peak = jnp.maximum(peak, top + bias)
-        ps[0 : 6 * W] = scores[0 : 6 * W]
-        ps[6 * W :] = seen
+        queries = joined(s.qb, o, h, b, g)
+        bias = biases(o, b)
+        peak = None
+        for lo, hi in CUTS:
+            scores = nt(s.ku[t, lo * W : hi * W], queries)
+            for i in range(lo, hi):
+                part = scores[(i - lo) * W : (i + 1 - lo) * W]
+                if i == 6:
+                    part = part + twice(s.mb[o, b])
+                ps[i * W : (i + 1) * W] = part
+                top = jnp.max(part, axis=0, keepdims=True)
+                if i < 6:
+                    top = top + bias[i]
+                peak = top if peak is None else jnp.maximum(peak, top)
         pk[0:1] = peak * exp_scale
 
     def soften(j, h, ps, pk, low, do):
@@ -397,28 +415,34 @@
 
     def attend(j, h, low, do):
         t, o, b, g = chunk(j, h)
-        attended = jnp.transpose(nn(s.vt[t], low[...])).astype(BF16)
-        s.acc[t] += nn(low[...], do[...])
+        attended = [nn(s.vt[t, :, lo * W : hi * W], low[lo * W : hi * W]) for lo, hi in CUTS]
+        attended = jnp.transpose(attended[0] + attended[1]).astype(BF16)
+        for lo, hi in CUTS:
+            s.acc[t, lo * W : hi * W] += nn(low[lo * W : hi * W], do[...])
         for i, x in enumerate(pair(s.ob, o, h, b, g)):
             x[...] = attended[i * W : (i + 1) * W]
         product = do[...].astype(F32) * attended.astype(F32)
         s.dl[j, 0:1] = jnp.sum(jnp.transpose(product), axis=0, keepdims=True)
 
     def forward(h):
-        def prepare(t, carry):
-            gather_block(t, h, K_, s.ku)
-            gather_block(t, h, V_, s.vu)
-            s.kt[t] = jnp.transpose(s.ku[t])
-            s.vt[t] = jnp.transpose(s.vu[t])
-            return carry
-
-        lax.fori_loop(0, 4, prepare, 0)
-        s.acc[...] = jnp.zeros_like(s.acc)
+        def prepare(kv, whole, turned):
+            await_bytes(s.kvp.at[kv, h, pl.ds(0, 2)], s.kv_relay.at[kv, h])
+
+            def step(t, carry):
+                gather_block(t, h, kv, whole)
+                turned[t] = jnp.transpose(whole[t])
+                return carry
+
+            lax.fori_loop(0, 4, step, 0)
+
         even, odd = (s.ps0, s.pk0), (s.ps1, s.pk1)
         low_even, low_odd = (s.low0, s.do0), (s.low1, s.do1)
+        prepare(K_, s.ku, s.kt)
         score(0, h, *even)
         score(1, h, *odd)
         soften(0, h, *even, *low_even)
+        s.acc[...] = jnp.zeros_like(s.acc)
+        prepare(V_, s.vu, s.vt)
 
         def step(i, carry):
             j = 2 * i
@@ -438,13 +462,19 @@
 
     def score_grad(j, h, low):
         t, o, b, g = chunk(j, h)
-        dprobs = nt(s.vu[t], s.do[j])
-        low[...] = (s.pf[j] * (dprobs - s.dl[j, 0:1]) * inv_root).astype(BF16)
+        delta = s.dl[j, 0:1]
+        for lo, hi in CUTS:
+            rows = pl.ds(lo * W, (hi - lo) * W)
+            dprobs = nt(s.vu[t, rows], s.do[j])
+            low[rows] = (s.pf[j, rows] * (dprobs - delta) * inv_root).astype(BF16)
 
     def input_grads(j, h, low):
         t, o, b, g = chunk(j, h)
-        grad = jnp.transpose(nn(s.kt[t], low[...])).astype(BF16)
-        s.acc[t] += nn(low[...], joined(s.qb, o, h, b, g))
+        grad = [nn(s.kt[t, :, lo * W : hi * W], low[lo * W : hi * W]) for lo, hi in CUTS]
+        grad = jnp.transpose(grad[0] + grad[1]).astype(BF16)
+        queries = joined(s.qb, o, h, b, g)
+        for lo, hi in CUTS:
+            s.acc[t, lo * W : hi * W] += nn(low[lo * W : hi * W], queries)
         for i, x in enumerate(pair(s.gb, o, h, b, g)):
             x[...] = grad[i * W : (i + 1) * W]
 
@@ -533,14 +563,16 @@
 
     for h in range(2):
         await_bytes(s.gath.at[h, pl.ds(0, chips - 1)], s.pr_recv.at[1, h])
-        for kv in range(2):
-            await_bytes(s.kvp.at[kv, h, pl.ds(0, 4)], s.kv_recv.at[kv, h])
-            await_bytes((s.qb, s.ub)[kv].at[other, h], s.qu_recv.at[h, kv])
-            own_qu[h][kv].wait()
+        for i in range(2):
+            await_bytes((s.qb, s.ub)[i].at[other, h], s.qu_recv.at[h, i])
+            own_qu[h][i].wait()
         clear()
         forward(h)
         send_grads(V_, h)
         send_rows(s.ob, attn, h, s.out_recv.at[0, h])
+        if h == 0:
+            relay_chain(1, K_)
+            relay_chain(1, V_)
         if h == 1:
             sum_prompt(K_, 0)
         clear()

time: 86.1 us -> 87.1 us (1.012)
  the two profiles are of different devices: /device:TPU:1 before, /device:TPU:33 now
where the time goes in v4:
time: 87.1 us; the launch traced here: 86.9 us
  Pallas kernels  86.3 us (99%)
    pallas_call x1, Pallas kernels, body(): pl.pallas_call(functools.partial(kernel, lax.axis_size('dp'), lax.axis_si...  83.9 us
    pallas_call x1, Pallas kernels, body(): pl.pallas_call(write_out, out_shape=[jax.ShapeDtypeStruct(x.shape, x.dtyp...  2.37 us

profile of v4, /device:TPU:33, one launch (start us, length us, event | category | flops | bytes accessed | tf_op | source)
XLA Modules:
  0.0 86.9 jit_solution(3261328191427032086)
XLA Ops:
  0.6 83.9 %shard_map.120 = (bf16[256,4096]{1,0:T(8,128)(2,1)S(1)}, bf16[256,4096]{1,0:T(8,128)(2,1)S(1)}, f32[256,512]{1,0:T(8,128)S(1)}, f32[256,512]{1,0:T(8,128)S(1)}) custom-call(bf16[256,4096]{1,0:T(8,128)(2,1)} %q.1, bf16[256,512]{1,0:T(8,128)(2,1)} %k.1, bf16[256,512]{1,0:T(8,128)(2,1)} %v.1, bf16[256,4096]{1,0:T(8,128)(2,1)} %u.1, s32[2,6]{1,0:T(2,128)} %anc.1, ...), custom_call_target="tpu_custom_call" | custom-call | tf_op jit(solution)/shard_map/pallas_call | solution.py:617
  84.6 2.4 %shard_map.121 = (bf16[256,4096]{1,0:T(8,128)(2,1)}, bf16[256,4096]{1,0:T(8,128)(2,1)}, f32[256,512]{1,0:T(8,128)}, f32[256,512]{1,0:T(8,128)}) custom-call(bf16[256,4096]{1,0:T(8,128)(2,1)S(1)} %get-tuple-element.8.refs_0_, bf16[256,4096]{1,0:T(8,128)(2,1)S(1)} %get-tuple-element.9.refs_1_, f32[256,512]{1,0:T(8,128)S(1)} %get-tuple-element.10.refs_2_, ...), custom_call_target="tpu_custom_call" | custom-call | tf_op jit(solution)/shard_map/pallas_call | solution.py:642

commit v5 on v4

--- a/solution.py
+++ b/solution.py
@@ -15,6 +15,8 @@
 R = 8
 C = R * W
 N = 7 * W
+H = 4
+M = H * W
 HOPS = 4
 K_, V_ = 0, 1
 CUTS = ((0, 4), (4, 7))
@@ -26,10 +28,6 @@
 
 def nt(a, b):
     return lax.dot_general(a, b, (((1,), (1,)), ((), ())), preferred_element_type=F32)
-
-
-def tn(a, b):
-    return lax.dot_general(a, b, (((0,), (0,)), ((), ())), preferred_element_type=F32)
 
 
 SCRATCH = dict(
@@ -51,18 +49,19 @@
     vu=pltpu.VMEM((4, N, W), BF16),
     kt=pltpu.VMEM((4, W, N), BF16),
     vt=pltpu.VMEM((4, W, N), BF16),
-    pf=pltpu.VMEM((16, N, 2 * W), F32),
-    dl=pltpu.VMEM((16, 8, 2 * W), F32),
-    do=pltpu.VMEM((16, 2 * W, W), BF16),
-    ps0=pltpu.VMEM((N, 2 * W), F32),
-    ps1=pltpu.VMEM((N, 2 * W), F32),
-    pk0=pltpu.VMEM((8, 2 * W), F32),
-    pk1=pltpu.VMEM((8, 2 * W), F32),
-    low0=pltpu.VMEM((N, 2 * W), BF16),
-    low1=pltpu.VMEM((N, 2 * W), BF16),
-    do0=pltpu.VMEM((2 * W, W), BF16),
-    do1=pltpu.VMEM((2 * W, W), BF16),
-    acc=pltpu.VMEM((4, N, W), F32),
+    qt=pltpu.VMEM((8, W, M), BF16),
+    dt=pltpu.VMEM((8, W, M), BF16),
+    pf=pltpu.VMEM((8, N, M), F32),
+    dl=pltpu.VMEM((8, 8, M), F32),
+    ps0=pltpu.VMEM((N, M), F32),
+    ps1=pltpu.VMEM((N, M), F32),
+    pk0=pltpu.VMEM((8, M), F32),
+    pk1=pltpu.VMEM((8, M), F32),
+    low0=pltpu.VMEM((N, M), BF16),
+    low1=pltpu.VMEM((N, M), BF16),
+    do0=pltpu.VMEM((W, M), BF16),
+    do1=pltpu.VMEM((W, M), BF16),
+    acc=pltpu.VMEM((4, W, N), F32),
     gacc=pltpu.VMEM((6, T, W), F32),
     pacc=pltpu.VMEM((T, W), F32),
     own=pltpu.VMEM((2, 2, T, W), F32),
@@ -336,33 +335,31 @@
     def spread_blocks(h):
         def step(t, carry):
             o, b = where_is(t, h)
-            s.pacc[...] += s.acc[t, 0 : 2 * W]
+            x = jnp.transpose(s.acc[t])
+            s.pacc[...] += x[0 : 2 * W]
             for i in range(HOPS):
                 chosen = jnp.broadcast_to(s.meta[o, b, 5 - i : 6 - i, :], (W, W)) == 1
-                x = s.acc[t, (2 + i) * W : (3 + i) * W]
-                s.gacc[o + i, 0:W] += jnp.where(chosen, 0.0, x)
-                s.gacc[o + i, W:] += jnp.where(chosen, x, 0.0)
-            s.gacc[o + 4, pl.ds(pl.multiple_of(b * W, W), W), :] += s.acc[t, 6 * W :]
+                y = x[(2 + i) * W : (3 + i) * W]
+                s.gacc[o + i, 0:W] += jnp.where(chosen, 0.0, y)
+                s.gacc[o + i, W:] += jnp.where(chosen, y, 0.0)
+            s.gacc[o + 4, pl.ds(pl.multiple_of(b * W, W), W), :] += x[6 * W :]
             return carry
 
         lax.fori_loop(0, 4, step, 0)
 
     def chunk(j, h):
-        t = j // 4
+        t = j // 2
         o, b = where_is(t, h)
-        return t, o, b, lax.rem(j, 4)
-
-    def pair(ref, o, h, b, g):
+        return t, o, b, lax.rem(j, 2)
+
+    def heads(ref, o, h, b, g):
         rows = pl.ds(pl.multiple_of(b * W, W), W)
         return [
-            ref.at[o, h, rows, pl.ds(pl.multiple_of((2 * g + i) * W, W), W)] for i in range(2)
+            ref.at[o, h, rows, pl.ds(pl.multiple_of((H * g + i) * W, W), W)] for i in range(H)
         ]
 
-    def joined(ref, o, h, b, g):
-        return jnp.concatenate([x[...] for x in pair(ref, o, h, b, g)], axis=0)
-
-    def twice(row):
-        return jnp.concatenate([row, row], axis=1)
+    def across(row):
+        return jnp.concatenate([row] * H, axis=1)
 
     META_ROWS = (0, 1, 5, 4, 3, 2)
 
@@ -371,20 +368,21 @@
         for i in range(6):
             row = s.meta[o, b, META_ROWS[i] : META_ROWS[i] + 1, :]
             unseen = row <= 0 if i < 2 else row < 0
-            rows.append(twice(jnp.where(unseen, -jnp.inf, 0.0)))
+            rows.append(across(jnp.where(unseen, -jnp.inf, 0.0)))
         return rows
 
     def score(j, h, ps, pk):
         t, o, b, g = chunk(j, h)
-        queries = joined(s.qb, o, h, b, g)
+        queries = jnp.concatenate([jnp.transpose(x[...]) for x in heads(s.qb, o, h, b, g)], axis=1)
+        s.qt[j] = queries
         bias = biases(o, b)
         peak = None
         for lo, hi in CUTS:
-            scores = nt(s.ku[t, lo * W : hi * W], queries)
+            scores = nn(s.ku[t, lo * W : hi * W], queries)
             for i in range(lo, hi):
                 part = scores[(i - lo) * W : (i + 1 - lo) * W]
                 if i == 6:
-                    part = part + twice(s.mb[o, b])
+                    part = part + across(s.mb[o, b])
                 ps[i * W : (i + 1) * W] = part
                 top = jnp.max(part, axis=0, keepdims=True)
                 if i < 6:
@@ -396,7 +394,7 @@
         t, o, b, g = chunk(j, h)
         shift = pk[0:1]
         bias = biases(o, b)
-        denominator = jnp.zeros((1, 2 * W), F32)
+        denominator = jnp.zeros((1, M), F32)
         for i in range(7):
             here = shift if i == 6 else shift - bias[i]
             e = jnp.exp2(ps[i * W : (i + 1) * W] * exp_scale - here)
@@ -408,21 +406,22 @@
             s.pf[j, i * W : (i + 1) * W] = probs
             low[i * W : (i + 1) * W] = probs.astype(BF16)
         weight = s.wt[o, b]
-        up = [x[...].astype(F32) * weight for x in pair(s.ub, o, h, b, g)]
-        grad_out = jnp.concatenate(up, axis=0).astype(BF16)
+        up = [
+            jnp.transpose((x[...].astype(F32) * weight).astype(BF16))
+            for x in heads(s.ub, o, h, b, g)
+        ]
+        grad_out = jnp.concatenate(up, axis=1)
         do[...] = grad_out
-        s.do[j] = grad_out
+        s.dt[j] = grad_out
 
     def attend(j, h, low, do):
         t, o, b, g = chunk(j, h)
-        attended = [nn(s.vt[t, :, lo * W : hi * W], low[lo * W : hi * W]) for lo, hi in CUTS]
-        attended = jnp.transpose(attended[0] + attended[1]).astype(BF16)
-        for lo, hi in CUTS:
-            s.acc[t, lo * W : hi * W] += nn(low[lo * W : hi * W], do[...])
-        for i, x in enumerate(pair(s.ob, o, h, b, g)):
-            x[...] = attended[i * W : (i + 1) * W]
+        attended = nn(s.vt[t], low[...]).astype(BF16)
+        s.acc[t] += nt(do[...], low[...])
+        for i, x in enumerate(heads(s.ob, o, h, b, g)):
+            x[...] = jnp.transpose(attended[:, i * W : (i + 1) * W])
         product = do[...].astype(F32) * attended.astype(F32)
-        s.dl[j, 0:1] = jnp.sum(jnp.transpose(product), axis=0, keepdims=True)
+        s.dl[j, 0:1] = jnp.sum(product, axis=0, keepdims=True)
 
     def forward(h):
         def prepare(kv, whole, turned):
@@ -446,6 +445,12 @@
 
         def step(i, carry):
             j = 2 * i
+            if h == 0:
+
+                @pl.when(i == 2)
+                def _():
+                    await_mate(h)
+
             attend(j - 2, h, *low_even)
             score(j, h, *even)
             soften(j - 1, h, *odd, *low_odd)
@@ -454,29 +459,30 @@
             soften(j, h, *even, *low_even)
             return carry
 
-        lax.fori_loop(1, 8, step, 0)
-        attend(14, h, *low_even)
-        soften(15, h, *odd, *low_odd)
-        attend(15, h, *low_odd)
+        lax.fori_loop(1, 4, step, 0)
+        attend(6, h, *low_even)
+        soften(7, h, *odd, *low_odd)
+        attend(7, h, *low_odd)
         spread_blocks(h)
 
+    def await_mate(h):
+        for i in range(2):
+            await_bytes((s.qb, s.ub)[i].at[other, h], s.qu_recv.at[h, i])
+
     def score_grad(j, h, low):
-        t, o, b, g = chunk(j, h)
+        t = j // 2
         delta = s.dl[j, 0:1]
         for lo, hi in CUTS:
             rows = pl.ds(lo * W, (hi - lo) * W)
-            dprobs = nt(s.vu[t, rows], s.do[j])
+            dprobs = nn(s.vu[t, rows], s.dt[j])
             low[rows] = (s.pf[j, rows] * (dprobs - delta) * inv_root).astype(BF16)
 
     def input_grads(j, h, low):
         t, o, b, g = chunk(j, h)
-        grad = [nn(s.kt[t, :, lo * W : hi * W], low[lo * W : hi * W]) for lo, hi in CUTS]
-        grad = jnp.transpose(grad[0] + grad[1]).astype(BF16)
-        queries = joined(s.qb, o, h, b, g)
-        for lo, hi in CUTS:
-            s.acc[t, lo * W : hi * W] += nn(low[lo * W : hi * W], queries)
-        for i, x in enumerate(pair(s.gb, o, h, b, g)):
-            x[...] = grad[i * W : (i + 1) * W]
+        grad = nn(s.kt[t], low[...]).astype(BF16)
+        s.acc[t] += nt(s.qt[j], low[...])
+        for i, x in enumerate(heads(s.gb, o, h, b, g)):
+            x[...] = jnp.transpose(grad[:, i * W : (i + 1) * W])
 
     def backward(h):
         s.acc[...] = jnp.zeros_like(s.acc)
@@ -490,10 +496,10 @@
             input_grads(j + 1, h, s.low1)
             return carry
 
-        lax.fori_loop(0, 7, step, 0)
-        score_grad(15, h, s.low1)
-        input_grads(14, h, s.low0)
-        input_grads(15, h, s.low1)
+        lax.fori_loop(0, 3, step, 0)
+        score_grad(7, h, s.low1)
+        input_grads(6, h, s.low0)
+        input_grads(7, h, s.low1)
         spread_blocks(h)
 
     def clear():
@@ -563,9 +569,10 @@
 
     for h in range(2):
         await_bytes(s.gath.at[h, pl.ds(0, chips - 1)], s.pr_recv.at[1, h])
-        for i in range(2):
-            await_bytes((s.qb, s.ub)[i].at[other, h], s.qu_recv.at[h, i])
-            own_qu[h][i].wait()
+        for copy in own_qu[h]:
+            copy.wait()
+        if h == 1:
+            await_mate(h)
         clear()
         forward(h)
         send_grads(V_, h)

time: 87.1 us -> 89.2 us (1.024)
  Pallas kernels: 86.3 us -> 88.3 us
    pallas_call x1, Pallas kernels: 83.9 us -> 85.9 us  [body(): pl.pallas_call(functools.partial(kernel, lax.axis_size('dp'), lax.axis_si...]
where the time goes in v5:
time: 89.2 us; the launch traced here: 89.1 us
  Pallas kernels  88.3 us (99%)
    pallas_call x1, Pallas kernels, body(): pl.pallas_call(functools.partial(kernel, lax.axis_size('dp'), lax.axis_si...  85.9 us
    pallas_call x1, Pallas kernels, body(): pl.pallas_call(write_out, out_shape=[jax.ShapeDtypeStruct(x.shape, x.dtyp...  2.37 us

profile of v5, /device:TPU:33, one launch (start us, length us, event | category | flops | bytes accessed | tf_op | source)
XLA Modules:
  0.0 89.1 jit_solution(17632610339473350337)
XLA Ops:
  0.6 85.9 %shard_map.120 = (bf16[256,4096]{1,0:T(8,128)(2,1)S(1)}, bf16[256,4096]{1,0:T(8,128)(2,1)S(1)}, f32[256,512]{1,0:T(8,128)S(1)}, f32[256,512]{1,0:T(8,128)S(1)}) custom-call(bf16[256,4096]{1,0:T(8,128)(2,1)} %q.1, bf16[256,512]{1,0:T(8,128)(2,1)} %k.1, bf16[256,512]{1,0:T(8,128)(2,1)} %v.1, bf16[256,4096]{1,0:T(8,128)(2,1)} %u.1, s32[2,6]{1,0:T(2,128)} %anc.1, ...), custom_call_target="tpu_custom_call" | custom-call | tf_op jit(solution)/shard_map/pallas_call | solution.py:624
  86.6 2.4 %shard_map.121 = (bf16[256,4096]{1,0:T(8,128)(2,1)}, bf16[256,4096]{1,0:T(8,128)(2,1)}, f32[256,512]{1,0:T(8,128)}, f32[256,512]{1,0:T(8,128)}) custom-call(bf16[256,4096]{1,0:T(8,128)(2,1)S(1)} %get-tuple-element.8.refs_0_, bf16[256,4096]{1,0:T(8,128)(2,1)S(1)} %get-tuple-element.9.refs_1_, f32[256,512]{1,0:T(8,128)S(1)} %get-tuple-element.10.refs_2_, ...), custom_call_target="tpu_custom_call" | custom-call | tf_op jit(solution)/shard_map/pallas_call | solution.py:649

commit v6 on v4

--- a/solution.py
+++ b/solution.py
@@ -28,21 +28,16 @@
     return lax.dot_general(a, b, (((1,), (1,)), ((), ())), preferred_element_type=F32)
 
 
-def tn(a, b):
-    return lax.dot_general(a, b, (((0,), (0,)), ((), ())), preferred_element_type=F32)
-
-
 SCRATCH = dict(
     kvp=pltpu.VMEM((2, 2, 6, T, W), BF16),
     qb=pltpu.VMEM((2, 2, T, C), BF16),
     ub=pltpu.VMEM((2, 2, T, C), BF16),
     ob=pltpu.VMEM((2, 2, T, C), BF16),
     gb=pltpu.VMEM((2, 2, T, C), BF16),
-    cand=pltpu.VMEM((2, 16, 2, 16, W), BF16),
-    scat0=pltpu.VMEM((16, 2, 16, W), BF16),
-    scat1=pltpu.VMEM((16, 2, 16, W), BF16),
+    cand=pltpu.VMEM((16, 2, 2, 16, W), BF16),
+    scat=pltpu.VMEM((16, 2, 2, 16, W), BF16),
     sel=pltpu.VMEM((2, 2, 16, W), BF16),
-    gath=pltpu.VMEM((2, 16, 2, 16, W), BF16),
+    gath=pltpu.VMEM((16, 2, 2, 16, W), BF16),
     meta=pltpu.VMEM((2, 2, 8, W), jnp.int32),
     lens=pltpu.VMEM((4, 8, W), jnp.int32),
     wt=pltpu.VMEM((2, 2, W, W), F32),
@@ -70,10 +65,10 @@
     mrecv=pltpu.VMEM((2, 2, T, W), F32),
     gsend=pltpu.VMEM((2, 2, 4, T, W), BF16),
     grecv=pltpu.VMEM((2, 2, 2, 2, T, W), BF16),
-    psend=pltpu.VMEM((2, 2, 16, 16, W), BF16),
-    prec=pltpu.VMEM((2, 2, 16, 16, W), BF16),
+    psend=pltpu.VMEM((2, 16, 2, 16, W), BF16),
+    prec=pltpu.VMEM((2, 16, 2, 16, W), BF16),
     agsend=pltpu.VMEM((2, 2, 16, W), BF16),
-    ag=pltpu.VMEM((2, 2, 32, 16, W), BF16),
+    ag=pltpu.VMEM((2, 32, 2, 16, W), BF16),
     one_send=pltpu.SemaphoreType.DMA((64,)),
     local=pltpu.SemaphoreType.DMA((12,)),
     kv_recv=pltpu.SemaphoreType.DMA((2, 2)),
@@ -84,14 +79,15 @@
     lens_recv=pltpu.SemaphoreType.DMA,
     qu_recv=pltpu.SemaphoreType.DMA((2, 2)),
     out_recv=pltpu.SemaphoreType.DMA((2, 2)),
-    pr_send=pltpu.SemaphoreType.DMA((2, 2)),
-    pr_recv=pltpu.SemaphoreType.DMA((2, 2)),
+    pr_send=pltpu.SemaphoreType.DMA((2,)),
+    pr_recv=pltpu.SemaphoreType.DMA((2,)),
     g_recv=pltpu.SemaphoreType.DMA((2, 2)),
     m_recv=pltpu.SemaphoreType.DMA((2, 2)),
-    ps_send=pltpu.SemaphoreType.DMA((2, 2)),
-    ps_recv=pltpu.SemaphoreType.DMA((2, 2)),
-    ag_send=pltpu.SemaphoreType.DMA((2, 2)),
-    ag_recv=pltpu.SemaphoreType.DMA((2, 2)),
+    ps_send=pltpu.SemaphoreType.DMA((2,)),
+    ps_recv=pltpu.SemaphoreType.DMA((2,)),
+    ag_send=pltpu.SemaphoreType.DMA((2,)),
+    ag_recv=pltpu.SemaphoreType.DMA((2,)),
+    ag_mate=pltpu.SemaphoreType.DMA((2,)),
 )
 
 
@@ -116,7 +112,6 @@
     root_chip, root_core = lax.div(root, 2), lax.rem(root, 2)
 
     sends = []
-    scat = (s.scat0, s.scat1)
 
     def send(src, dst, recv_sem, to):
         copy = pltpu.make_async_remote_copy(
@@ -135,13 +130,17 @@
 
     barrier = pltpu.get_barrier_semaphore()
 
-    def greet(i, carry):
-        pl.semaphore_signal(
-            barrier, inc=1, device_id={"ctx": lax.rem(me + i, ring)}, device_id_type=MESH
-        )
+    def greet(to):
+        pl.semaphore_signal(barrier, inc=1, device_id={"ctx": to}, device_id_type=MESH)
+
+    def greet_chip(i, carry):
+        greet(2 * lax.rem(chip + i, chips) + core)
         return carry
 
-    lax.fori_loop(1, ring, greet, 0)
+    lax.fori_loop(1, chips, greet_chip, 0)
+    greet(mate)
+    for i in (1, 2, chips - 2, chips - 1):
+        greet(2 * lax.rem(chip + i, chips) + other)
     for i in range(1, groups):
         pl.semaphore_signal(
             barrier, inc=1, device_id={"dp": lax.rem(z + i, groups)}, device_id_type=MESH
@@ -192,7 +191,7 @@
         s.meta[core, b, 6:7, :] = seg[b : b + 1, :]
         s.meta[core, b, 7:8, :] = resp[b : b + 1, :]
 
-    pl.semaphore_wait(barrier, ring - 1 + groups - 1)
+    pl.semaphore_wait(barrier, chips - 1 + 1 + 4 + groups - 1)
 
     for h in range(2):
         for kv, src in ((K_, k), (V_, v)):
@@ -255,20 +254,14 @@
     for h in range(2):
         for kv in range(2):
             x = lax.select(root_core == 0, s.kvp[kv, h, 4], s.kvp[kv, h, 5])
-            s.cand[h, :, kv] = x.reshape(16, 16, W)
-        scat[h][chip] = s.cand[h, chip]
-        to_chips(
-            lambda c, h=h: loop_send(
-                s.cand.at[h, c],
-                scat[h].at[chip],
-                s.pr_send.at[0, h],
-                s.pr_recv.at[0, h],
-                2 * c + core,
-            )
+            s.cand[:, h, kv] = x.reshape(16, 16, W)
+    s.scat[chip] = s.cand[chip]
+    to_chips(
+        lambda c: loop_send(
+            s.cand.at[c], s.scat.at[chip], s.pr_send.at[0], s.pr_recv.at[0], 2 * c + core
         )
-        if h == 0:
-            send_chain(0, V_)
-    send_qu(0)
+    )
+    send_chain(0, V_)
 
     await_bytes(s.meta.at[0], s.meta_recv)
     await_bytes(s.lens.at[pl.ds(0, groups - 1)], s.lens_recv)
@@ -299,23 +292,16 @@
             seen = seen | (key_row == query_col)
             s.mb[o, b] = jnp.where(seen, 0.0, -jnp.inf)
 
-    for h in range(2):
-        await_bytes(scat[h].at[pl.ds(0, chips - 1)], s.pr_recv.at[0, h])
-        prompt_slice = scat[h][root_chip]
-        s.sel[h] = prompt_slice
-        s.gath[h, chip] = prompt_slice
-        to_chips(
-            lambda c, h=h: loop_send(
-                s.sel.at[h],
-                s.gath.at[h, chip],
-                s.pr_send.at[1, h],
-                s.pr_recv.at[1, h],
-                2 * c + core,
-            )
-        )
-        if h == 0:
-            relay_chain(0, K_)
-            relay_chain(0, V_)
+    await_bytes(s.scat.at[pl.ds(0, chips - 1)], s.pr_recv.at[0])
+    prompt_slice = s.scat[root_chip]
+    s.sel[...] = prompt_slice
+    s.gath[chip] = prompt_slice
+    to_chips(
+        lambda c: loop_send(s.sel, s.gath.at[chip], s.pr_send.at[1], s.pr_recv.at[1], 2 * c + core)
+    )
+    relay_chain(0, K_)
+    relay_chain(0, V_)
+    send_qu(0)
     for kv in range(2):
         send_chain(1, kv)
     send_qu(1)
@@ -325,7 +311,7 @@
 
     def gather_block(t, h, kv, to):
         o, b = where_is(t, h)
-        to[t, 0 : 2 * W] = s.gath[h, :, kv].reshape(T, W)
+        to[t, 0 : 2 * W] = s.gath[:, h, kv].reshape(T, W)
         for i in range(HOPS):
             chosen = s.meta[o, b, 5 - i : 6 - i, :]
             both = s.kvp[kv, h, o + i].astype(F32)
@@ -446,6 +432,12 @@
 
         def step(i, carry):
             j = 2 * i
+            if h == 0:
+
+                @pl.when(i == 4)
+                def _():
+                    await_mate(h)
+
             attend(j - 2, h, *low_even)
             score(j, h, *even)
             soften(j - 1, h, *odd, *low_odd)
@@ -459,6 +451,10 @@
         soften(15, h, *odd, *low_odd)
         attend(15, h, *low_odd)
         spread_blocks(h)
+
+    def await_mate(h):
+        for i in range(2):
+            await_bytes((s.qb, s.ub)[i].at[other, h], s.qu_recv.at[h, i])
 
     def score_grad(j, h, low):
         t, o, b, g = chunk(j, h)
@@ -501,17 +497,18 @@
         s.pacc[...] = jnp.zeros_like(s.pacc)
 
     def send_grads(kv, h):
-        s.psend[kv, h] = s.pacc[...].reshape(16, 16, W).astype(BF16)
-        to_chips(
-            lambda c: loop_send(
-                s.psend.at[kv, h, c],
-                s.prec.at[kv, h, chip],
-                s.ps_send.at[kv, h],
-                s.ps_recv.at[kv, h],
-                2 * c + core,
+        s.psend[h, :, kv] = s.pacc[...].reshape(16, 16, W).astype(BF16)
+        if kv == K_:
+            s.prec[h, chip] = s.psend[h, chip]
+            to_chips(
+                lambda c: loop_send(
+                    s.psend.at[h, c],
+                    s.prec.at[h, chip],
+                    s.ps_send.at[h],
+                    s.ps_recv.at[h],
+                    2 * c + core,
+                )
             )
-        )
-        s.prec[kv, h, chip] = s.psend[kv, h, chip]
         for i in range(4):
             s.gsend[kv, h, i] = s.gacc[i].astype(BF16)
             hop = 2 if i < 2 else 1
@@ -531,41 +528,46 @@
         send(staged.at[other, h], out.at[:, qcols(core, h)], recv_sem, mate)
         own_out.append(fetch(staged.at[core, h], out.at[:, qcols(core, h)]))
 
-    def sum_prompt(kv, h):
-        await_bytes(s.prec.at[kv, h, pl.ds(0, chips - 1)], s.ps_recv.at[kv, h])
-        summed = jnp.sum(s.prec[kv, h].astype(F32), axis=0).astype(BF16)
-        s.agsend[kv, h] = summed
-        s.ag[kv, h, 16 * core + chip] = summed
-
-        def step(i, carry):
-            loop_send(
-                s.agsend.at[kv, h],
-                s.ag.at[kv, h, 16 * core + chip],
-                s.ag_send.at[kv, h],
-                s.ag_recv.at[kv, h],
-                lax.rem(me + i, ring),
+    def sum_prompt(h):
+        await_bytes(s.prec.at[h, pl.ds(0, chips - 1)], s.ps_recv.at[h])
+        summed = jnp.sum(s.prec[h].astype(F32), axis=0).astype(BF16)
+        s.agsend[h] = summed
+        s.ag[h, 16 * core + chip] = summed
+        to_chips(
+            lambda c: loop_send(
+                s.agsend.at[h],
+                s.ag.at[h, 16 * core + chip],
+                s.ag_send.at[h],
+                s.ag_recv.at[h],
+                2 * c + core,
             )
-            return carry
-
-        lax.fori_loop(1, ring, step, 0)
+        )
+
+    def share_prompt(h):
+        await_bytes(s.ag.at[h, pl.ds(0, chips - 1)], s.ag_recv.at[h])
+        lane = pl.ds(16 * core, 16)
+        send(s.ag.at[h, lane], s.ag.at[h, lane], s.ag_mate.at[h], mate)
 
     def finish(kv, h):
         out = (gk, gv)[kv]
         await_bytes(s.grecv.at[kv, h], s.g_recv.at[kv, h])
         await_bytes(s.mrecv.at[kv, h], s.m_recv.at[kv, h])
-        await_bytes(s.ag.at[kv, h, pl.ds(0, ring - 1)], s.ag_recv.at[kv, h])
         for lane, mine in ((core, s.own), (other, s.mrecv)):
             x = mine[kv, h] + s.grecv[kv, h, 0, lane].astype(F32)
             x = x + s.grecv[kv, h, 1, lane].astype(F32)
-            prompt = s.ag[kv, h, pl.ds(16 * lane, 16)].astype(F32).reshape(T, W)
+            prompt = s.ag[h, pl.ds(16 * lane, 16), kv].astype(F32).reshape(T, W)
             here = jnp.full((T, W), root, jnp.int32) == me
             out[:, kcols(lane, h)] = x + jnp.where(here, prompt, 0.0)
 
+    def await_shared(h):
+        await_bytes(s.ag.at[h, pl.ds(0, chips)], s.ag_mate.at[h])
+
+    await_bytes(s.gath.at[pl.ds(0, chips - 1)], s.pr_recv.at[1])
     for h in range(2):
-        await_bytes(s.gath.at[h, pl.ds(0, chips - 1)], s.pr_recv.at[1, h])
-        for i in range(2):
-            await_bytes((s.qb, s.ub)[i].at[other, h], s.qu_recv.at[h, i])
-            own_qu[h][i].wait()
+        for copy in own_qu[h]:
+            copy.wait()
+        if h == 1:
+            await_mate(h)
         clear()
         forward(h)
         send_grads(V_, h)
@@ -573,17 +575,20 @@
         if h == 0:
             relay_chain(1, K_)
             relay_chain(1, V_)
-        if h == 1:
-            sum_prompt(K_, 0)
+        else:
+            sum_prompt(0)
         clear()
         backward(h)
         send_grads(K_, h)
-        sum_prompt(V_, h)
         send_rows(s.gb, gq, h, s.out_recv.at[1, h])
+    share_prompt(0)
+    sum_prompt(1)
+    await_shared(0)
     finish(V_, 0)
     finish(K_, 0)
+    share_prompt(1)
+    await_shared(1)
     finish(V_, 1)
-    sum_prompt(K_, 1)
     finish(K_, 1)
 
     for copy in own_out:
@@ -595,10 +600,9 @@
         copy.wait_send()
     await_bytes(s.lens.at[pl.ds(0, groups - 1)], s.lens_send)
     for i in range(2):
-        for h in range(2):
-            await_bytes(s.gath.at[h, pl.ds(0, chips - 1)], s.pr_send.at[i, h])
-            await_bytes(s.ag.at[i, h, pl.ds(0, ring - 1)], s.ag_send.at[i, h])
-            await_bytes(s.prec.at[i, h, pl.ds(0, chips - 1)], s.ps_send.at[i, h])
+        await_bytes(s.scat.at[pl.ds(0, chips - 1)], s.pr_send.at[i])
+        await_bytes(s.ag.at[i, pl.ds(0, chips - 1)], s.ag_send.at[i])
+        await_bytes(s.prec.at[i, pl.ds(0, chips - 1)], s.ps_send.at[i])
 
 
 def write_out(*refs):

time: 87.1 us -> 88.3 us (1.014)
  Pallas kernels: 86.3 us -> 87.5 us
    pallas_call x1, Pallas kernels: 83.9 us -> 85.1 us  [body(): pl.pallas_call(functools.partial(kernel, lax.axis_size('dp'), lax.axis_si...]
where the time goes in v6:
time: 88.3 us; the launch traced here: 88.1 us
  Pallas kernels  87.5 us (99%)
    pallas_call x1, Pallas kernels, body(): pl.pallas_call(functools.partial(kernel, lax.axis_size('dp'), lax.axis_si...  85.1 us
    pallas_call x1, Pallas kernels, body(): pl.pallas_call(write_out, out_shape=[jax.ShapeDtypeStruct(x.shape, x.dtyp...  2.37 us

profile of v6, /device:TPU:33, one launch (start us, length us, event | category | flops | bytes accessed | tf_op | source)
XLA Modules:
  0.0 88.1 jit_solution(15744792511140108845)
XLA Ops:
  0.6 85.1 %shard_map.120 = (bf16[256,4096]{1,0:T(8,128)(2,1)S(1)}, bf16[256,4096]{1,0:T(8,128)(2,1)S(1)}, f32[256,512]{1,0:T(8,128)S(1)}, f32[256,512]{1,0:T(8,128)S(1)}) custom-call(bf16[256,4096]{1,0:T(8,128)(2,1)} %q.1, bf16[256,512]{1,0:T(8,128)(2,1)} %k.1, bf16[256,512]{1,0:T(8,128)(2,1)} %v.1, bf16[256,4096]{1,0:T(8,128)(2,1)} %u.1, s32[2,6]{1,0:T(2,128)} %anc.1, ...), custom_call_target="tpu_custom_call" | custom-call | tf_op jit(solution)/shard_map/pallas_call | solution.py:621
  85.8 2.4 %shard_map.121 = (bf16[256,4096]{1,0:T(8,128)(2,1)}, bf16[256,4096]{1,0:T(8,128)(2,1)}, f32[256,512]{1,0:T(8,128)}, f32[256,512]{1,0:T(8,128)}) custom-call(bf16[256,4096]{1,0:T(8,128)(2,1)S(1)} %get-tuple-element.8.refs_0_, bf16[256,4096]{1,0:T(8,128)(2,1)S(1)} %get-tuple-element.9.refs_1_, f32[256,512]{1,0:T(8,128)S(1)} %get-tuple-element.10.refs_2_, ...), custom_call_target="tpu_custom_call" | custom-call | tf_op jit(solution)/shard_map/pallas_call | solution.py:646

commit v7 on v6

--- a/solution.py
+++ b/solution.py
@@ -57,7 +57,10 @@
     low1=pltpu.VMEM((N, 2 * W), BF16),
     do0=pltpu.VMEM((2 * W, W), BF16),
     do1=pltpu.VMEM((2 * W, W), BF16),
+    ds0=pltpu.VMEM((N, 2 * W), BF16),
+    ds1=pltpu.VMEM((N, 2 * W), BF16),
     acc=pltpu.VMEM((4, N, W), F32),
+    kacc=pltpu.VMEM((4, N, W), F32),
     gacc=pltpu.VMEM((6, T, W), F32),
     pacc=pltpu.VMEM((T, W), F32),
     own=pltpu.VMEM((2, 2, T, W), F32),
@@ -319,16 +322,16 @@
             to[t, (2 + i) * W : (3 + i) * W] = picked.astype(BF16)
         to[t, 6 * W :] = s.kvp[kv, h, o + 4, pl.ds(pl.multiple_of(b * W, W), W), :]
 
-    def spread_blocks(h):
+    def spread_blocks(h, acc):
         def step(t, carry):
             o, b = where_is(t, h)
-            s.pacc[...] += s.acc[t, 0 : 2 * W]
+            s.pacc[...] += acc[t, 0 : 2 * W]
             for i in range(HOPS):
                 chosen = jnp.broadcast_to(s.meta[o, b, 5 - i : 6 - i, :], (W, W)) == 1
-                x = s.acc[t, (2 + i) * W : (3 + i) * W]
+                x = acc[t, (2 + i) * W : (3 + i) * W]
                 s.gacc[o + i, 0:W] += jnp.where(chosen, 0.0, x)
                 s.gacc[o + i, W:] += jnp.where(chosen, x, 0.0)
-            s.gacc[o + 4, pl.ds(pl.multiple_of(b * W, W), W), :] += s.acc[t, 6 * W :]
+            s.gacc[o + 4, pl.ds(pl.multiple_of(b * W, W), W), :] += acc[t, 6 * W :]
             return carry
 
         lax.fori_loop(0, 4, step, 0)
@@ -402,13 +405,14 @@
     def attend(j, h, low, do):
         t, o, b, g = chunk(j, h)
         attended = [nn(s.vt[t, :, lo * W : hi * W], low[lo * W : hi * W]) for lo, hi in CUTS]
-        attended = jnp.transpose(attended[0] + attended[1]).astype(BF16)
+        turned = (attended[0] + attended[1]).astype(BF16)
+        attended = jnp.transpose(turned)
         for lo, hi in CUTS:
             s.acc[t, lo * W : hi * W] += nn(low[lo * W : hi * W], do[...])
         for i, x in enumerate(pair(s.ob, o, h, b, g)):
             x[...] = attended[i * W : (i + 1) * W]
-        product = do[...].astype(F32) * attended.astype(F32)
-        s.dl[j, 0:1] = jnp.sum(jnp.transpose(product), axis=0, keepdims=True)
+        product = jnp.transpose(do[...]).astype(F32) * turned.astype(F32)
+        s.dl[j, 0:1] = jnp.sum(product, axis=0, keepdims=True)
 
     def forward(h):
         def prepare(kv, whole, turned):
@@ -449,8 +453,12 @@
         lax.fori_loop(1, 8, step, 0)
         attend(14, h, *low_even)
         soften(15, h, *odd, *low_odd)
+        s.kacc[...] = jnp.zeros_like(s.kacc)
+        score_grad(0, h, s.ds0)
         attend(15, h, *low_odd)
-        spread_blocks(h)
+        score_grad(1, h, s.ds1)
+        input_grads(0, h, s.ds0)
+        spread_blocks(h, s.acc)
 
     def await_mate(h):
         for i in range(2):
@@ -467,30 +475,25 @@
     def input_grads(j, h, low):
         t, o, b, g = chunk(j, h)
         grad = [nn(s.kt[t, :, lo * W : hi * W], low[lo * W : hi * W]) for lo, hi in CUTS]
-        grad = jnp.transpose(grad[0] + grad[1]).astype(BF16)
+        grad = jnp.transpose((grad[0] + grad[1]).astype(BF16))
         queries = joined(s.qb, o, h, b, g)
         for lo, hi in CUTS:
-            s.acc[t, lo * W : hi * W] += nn(low[lo * W : hi * W], queries)
+            s.kacc[t, lo * W : hi * W] += nn(low[lo * W : hi * W], queries)
         for i, x in enumerate(pair(s.gb, o, h, b, g)):
             x[...] = grad[i * W : (i + 1) * W]
 
     def backward(h):
-        s.acc[...] = jnp.zeros_like(s.acc)
-        score_grad(0, h, s.low0)
-
         def step(i, carry):
             j = 2 * i
-            score_grad(j + 1, h, s.low1)
-            input_grads(j, h, s.low0)
-            score_grad(j + 2, h, s.low0)
-            input_grads(j + 1, h, s.low1)
+            score_grad(j, h, s.ds0)
+            input_grads(j - 1, h, s.ds1)
+            score_grad(j + 1, h, s.ds1)
+            input_grads(j, h, s.ds0)
             return carry
 
-        lax.fori_loop(0, 7, step, 0)
-        score_grad(15, h, s.low1)
-        input_grads(14, h, s.low0)
-        input_grads(15, h, s.low1)
-        spread_blocks(h)
+        lax.fori_loop(1, 8, step, 0)
+        input_grads(15, h, s.ds1)
+        spread_blocks(h, s.kacc)
 
     def clear():
         s.gacc[...] = jnp.zeros_like(s.gacc)

time: 88.3 us -> 87.3 us (0.989)
  Pallas kernels: 87.5 us -> 86.2 us
    pallas_call x1, Pallas kernels: 85.1 us -> 83.8 us  [body(): pl.pallas_call(functools.partial(kernel, lax.axis_size('dp'), lax.axis_si...]
where the time goes in v7:
time: 87.3 us; the launch traced here: 86.8 us
  Pallas kernels  86.2 us (99%)
    pallas_call x1, Pallas kernels, body(): pl.pallas_call(functools.partial(kernel, lax.axis_size('dp'), lax.axis_si...  83.8 us
    pallas_call x1, Pallas kernels, body(): pl.pallas_call(write_out, out_shape=[jax.ShapeDtypeStruct(x.shape, x.dtyp...  2.37 us

profile of v7, /device:TPU:33, one launch (start us, length us, event | category | flops | bytes accessed | tf_op | source)
XLA Modules:
  0.0 86.8 jit_solution(3290301384119471452)
XLA Ops:
  0.6 83.8 %shard_map.120 = (bf16[256,4096]{1,0:T(8,128)(2,1)S(1)}, bf16[256,4096]{1,0:T(8,128)(2,1)S(1)}, f32[256,512]{1,0:T(8,128)S(1)}, f32[256,512]{1,0:T(8,128)S(1)}) custom-call(bf16[256,4096]{1,0:T(8,128)(2,1)} %q.1, bf16[256,512]{1,0:T(8,128)(2,1)} %k.1, bf16[256,512]{1,0:T(8,128)(2,1)} %v.1, bf16[256,4096]{1,0:T(8,128)(2,1)} %u.1, s32[2,6]{1,0:T(2,128)} %anc.1, ...), custom_call_target="tpu_custom_call" | custom-call | tf_op jit(solution)/shard_map/pallas_call | solution.py:624
  84.5 2.4 %shard_map.121 = (bf16[256,4096]{1,0:T(8,128)(2,1)}, bf16[256,4096]{1,0:T(8,128)(2,1)}, f32[256,512]{1,0:T(8,128)}, f32[256,512]{1,0:T(8,128)}) custom-call(bf16[256,4096]{1,0:T(8,128)(2,1)S(1)} %get-tuple-element.8.refs_0_, bf16[256,4096]{1,0:T(8,128)(2,1)S(1)} %get-tuple-element.9.refs_1_, f32[256,512]{1,0:T(8,128)S(1)} %get-tuple-element.10.refs_2_, ...), custom_call_target="tpu_custom_call" | custom-call | tf_op jit(solution)/shard_map/pallas_call | solution.py:649

commit v8 on v7

--- a/solution.py
+++ b/solution.py
@@ -17,7 +17,7 @@
 N = 7 * W
 HOPS = 4
 K_, V_ = 0, 1
-CUTS = ((0, 4), (4, 7))
+CUTS = ((0, 7),)
 
 
 def nn(a, b):
@@ -405,7 +405,7 @@
     def attend(j, h, low, do):
         t, o, b, g = chunk(j, h)
         attended = [nn(s.vt[t, :, lo * W : hi * W], low[lo * W : hi * W]) for lo, hi in CUTS]
-        turned = (attended[0] + attended[1]).astype(BF16)
+        turned = sum(attended[1:], attended[0]).astype(BF16)
         attended = jnp.transpose(turned)
         for lo, hi in CUTS:
             s.acc[t, lo * W : hi * W] += nn(low[lo * W : hi * W], do[...])
@@ -475,7 +475,7 @@
     def input_grads(j, h, low):
         t, o, b, g = chunk(j, h)
         grad = [nn(s.kt[t, :, lo * W : hi * W], low[lo * W : hi * W]) for lo, hi in CUTS]
-        grad = jnp.transpose((grad[0] + grad[1]).astype(BF16))
+        grad = jnp.transpose(sum(grad[1:], grad[0]).astype(BF16))
         queries = joined(s.qb, o, h, b, g)
         for lo, hi in CUTS:
             s.kacc[t, lo * W : hi * W] += nn(low[lo * W : hi * W], queries)

time: 87.3 us -> 88.1 us (level)
  Pallas kernels: 86.2 us -> 87.3 us
    pallas_call x1, Pallas kernels: 83.8 us -> 84.9 us  [body(): pl.pallas_call(functools.partial(kernel, lax.axis_size('dp'), lax.axis_si...]
where the time goes in v8:
time: 88.1 us; the launch traced here: 88 us
  Pallas kernels  87.3 us (99%)
    pallas_call x1, Pallas kernels, body(): pl.pallas_call(functools.partial(kernel, lax.axis_size('dp'), lax.axis_si...  84.9 us
    pallas_call x1, Pallas kernels, body(): pl.pallas_call(write_out, out_shape=[jax.ShapeDtypeStruct(x.shape, x.dtyp...  2.37 us

profile of v8, /device:TPU:33, one launch (start us, length us, event | category | flops | bytes accessed | tf_op | source)
XLA Modules:
  0.0 88.0 jit_solution(13147616888527069652)
XLA Ops:
  0.6 84.9 %shard_map.120 = (bf16[256,4096]{1,0:T(8,128)(2,1)S(1)}, bf16[256,4096]{1,0:T(8,128)(2,1)S(1)}, f32[256,512]{1,0:T(8,128)S(1)}, f32[256,512]{1,0:T(8,128)S(1)}) custom-call(bf16[256,4096]{1,0:T(8,128)(2,1)} %q.1, bf16[256,512]{1,0:T(8,128)(2,1)} %k.1, bf16[256,512]{1,0:T(8,128)(2,1)} %v.1, bf16[256,4096]{1,0:T(8,128)(2,1)} %u.1, s32[2,6]{1,0:T(2,128)} %anc.1, ...), custom_call_target="tpu_custom_call" | custom-call | tf_op jit(solution)/shard_map/pallas_call | solution.py:624
  85.6 2.4 %shard_map.121 = (bf16[256,4096]{1,0:T(8,128)(2,1)}, bf16[256,4096]{1,0:T(8,128)(2,1)}, f32[256,512]{1,0:T(8,128)}, f32[256,512]{1,0:T(8,128)}) custom-call(bf16[256,4096]{1,0:T(8,128)(2,1)S(1)} %get-tuple-element.8.refs_0_, bf16[256,4096]{1,0:T(8,128)(2,1)S(1)} %get-tuple-element.9.refs_1_, f32[256,512]{1,0:T(8,128)S(1)} %get-tuple-element.10.refs_2_, ...), custom_call_target="tpu_custom_call" | custom-call | tf_op jit(solution)/shard_map/pallas_call | solution.py:649
